TPU v7x, 128 devices: a whole 4x4x4 slice. The times are simulated.
128 devices in a mesh: az: 16 (over z_lo, x, core), wn: 8 (over y, z_hi).
Axes of the slice: x: 4, y: 4, z: 4 (z_hi: 2, z_lo: 2; z = z_hi * 2 + z_lo), core: 2. Of those that a mesh axis runs over, the one named last changes fastest.
Arguments:
- state: float32 [5, 32, 96, 2048], P(None, 'wn', None, 'az'), may hold values from -6 to 6
- base_flow: float32 [2, 32, 96], P(None, 'wn'), may hold values from -1 to 1
- az_scale: float32 [96], replicated, may hold values from 1 to 5
- blow_table: float32 [16], replicated, may hold values from 0.5 to 2
- seg_index: int32 [96, 2048], P(None, 'az'), may hold values from 0 to 15
- porous: int32 [96, 2048], P(None, 'az'), may hold values 0 or 1
Outputs:
- final_state: float32 [5, 32, 96, 2048], P(None, 'wn', None, 'az')
All inputs are finite; a program needn't handle non-finite values. No bound on the sum of `porous` on one device may be relied on, other than what follows from the above.
Results may differ from a plain program's by a relative error of at most 0.00002.
Values sent between devices are 32-bit elements; how exact they have to be, the bound alone decides.
No kernel may reach another device: no remote copies, remote signals or barrier semaphores. Data moves between devices by JAX's collectives and lax.ppermute only.
A program may use at most 128 MiB of HBM per device.

v0:
```python
import jax
import jax.numpy as jnp
from jax import lax
from jax.experimental import pallas as pl
from jax.experimental.pallas import tpu as pltpu
from jax.sharding import PartitionSpec as P

STEPS = 3
time_step = 0.25
viscosity = 0.05
heat_ratio = 1.4
admittance = 0.6

REACH = 12
OWN_T = 24
ROWS = OWN_T + 2 * REACH
SIDE = 32
SIGNS = (1.0, 1.0, -1.0, -1.0, 1.0)
VMEM = pl.BlockSpec(memory_space=pltpu.VMEM)
SMEM = pl.BlockSpec(memory_space=pltpu.SMEM)


def lane_of(shape):
    return lax.broadcasted_iota(jnp.int32, shape, len(shape) - 1)


def roll(x, shift):
    shift = shift % 128
    return pltpu.roll(x, shift, x.ndim - 1) if shift else x


def edges_kernel(table, state, seg, porous, walls, head, tail):
    seg_now = seg[...]
    blowing = jnp.zeros(seg_now.shape, jnp.float32)
    for k in range(16):
        blowing = jnp.where(seg_now == k, table[k], blowing)
    walls[0] = 2.0 * blowing
    walls[1] = porous[...].astype(jnp.float32)
    group = lane_of((96, 128)) // SIDE

    def pack(parts, start):
        out = jnp.zeros((96, 128), jnp.float32)
        for i, part in enumerate(parts):
            out = jnp.where(group == i, roll(part, SIDE * i - start), out)
        return out

    for c in range(5):
        parts = [state[c * 4 + l] for l in range(4)]
        head[c] = pack(parts, 0)
        tail[c] = pack(parts, 128 - SIDE)
    parts = [walls[0], walls[1]]
    head[5] = pack(parts, 0)
    tail[5] = pack(parts, 128 - SIDE)


def windows_kernel(place, state, walls, flow, before, after, pole, pieces, wall_window):
    quarter, half = place[0], place[1]

    def window(own, left, right, group):
        lane = lane_of(own.shape)
        first = jnp.where(lane < SIDE, roll(left, -SIDE * group), roll(own, SIDE))
        second = jnp.where(
            lane >= 128 - SIDE, roll(right, 128 - SIDE - SIDE * group), roll(own, -SIDE)
        )
        return first, second

    for c in range(5):
        for l in range(4):
            ch = c * 4 + l
            mine = window(state[ch], before[c], after[c], l)
            ghost = window(pole[ch], pole[22 + c], pole[28 + c], l)
            for h in range(2):
                pieces[h, ch, 0:12] = SIGNS[c] * ghost[h]
                pieces[h, ch, 12:48] = mine[h][0:36]
                pieces[2 + h, ch] = mine[h][12:60]
                pieces[4 + h, ch] = mine[h][36:84]
                pieces[6 + h, ch, 0:36] = mine[h][60:96]
                pieces[6 + h, ch, 36:48] = jnp.zeros((12, 128), jnp.float32)
    lane = lane_of((ROWS, 128))
    for l in range(4):
        for q in range(4):
            layer = flow[l, OWN_T * q : OWN_T * q + ROWS]
            for h in range(2):
                pieces[2 * q + h, l] = jnp.where(lane < 2, layer, pieces[2 * q + h, l])
    for k in range(2):
        mine = window(walls[k], before[5], after[5], k)
        ghost = window(pole[20 + k], pole[27], pole[33], k)
        mine = jnp.where(half == 0, mine[0], mine[1])
        ghost = jnp.where(half == 0, ghost[0], ghost[1])
        zeros = jnp.zeros((12, 128), jnp.float32)
        wall_window[k] = jnp.where(
            quarter == 0,
            jnp.concatenate([ghost, mine[0:36]], 0),
            jnp.where(
                quarter == 1,
                mine[12:60],
                jnp.where(quarter == 2, mine[36:84], jnp.concatenate([mine[60:96], zeros], 0)),
            ),
        )


def steps_kernel(start, metric, valid, wall, out, speed, buf_b, buf_c, buf_d):
    nu = viscosity
    lane = lane_of((8, 128))

    def spread(w, _):
        for l in range(4):
            layer = 0.5 * start[w * 20 + l]
            for k in range(2):
                speed[k, w * 4 + l] = jnp.broadcast_to(layer[:, k : k + 1], (ROWS, 128))
        return 0

    lax.fori_loop(0, 8, spread, 0)

    def stage_pass(source, base, target, scale, stage, last):
        low, high = stage, ROWS - stage

        def chunk(i, _):
            t0 = jnp.minimum(low + 8 * i, high - 8)
            here = pl.ds(t0, 8)
            m = metric[here, :]
            cm = scale * valid[here, :]
            ch = 0.5 * cm
            c_nu = nu * cm
            ca = (0.25 * c_nu) * (m * m)
            cc = -(4.0 * c_nu + 2.0 * ca)
            cmm = ch * m
            blow = wall[0, here, :]
            coated = wall[1, here, :] > 0.5

            def read(ref, w, c, l, rows=here):
                return ref[w * 20 + c * 4 + l, rows, :]

            def advance(w, carry):
                before, now = carry
                saved = []
                for l in range(4):
                    r = w * 4 + l + 1
                    if r < 32:
                        after = [read(source, r // 4, c, r % 4) for c in range(5)]
                    else:
                        after = [jnp.zeros((8, 128), jnp.float32)] * 5
                    down = [read(source, w, c, l, pl.ds(t0 - 1, 8)) for c in range(5)]
                    up = [read(source, w, c, l, pl.ds(t0 + 1, 8)) for c in range(5)]
                    hu = cm * speed[0, w * 4 + l, here, :]
                    hv = cm * speed[1, w * 4 + l, here, :]
                    rp, rm, tp, tm = c_nu - hu, c_nu + hu, c_nu - hv, c_nu + hv
                    dr_p = after[4] - before[4]
                    dt_p = up[4] - down[4]
                    da_p = roll(now[4], -1) - roll(now[4], 1)
                    div = (after[1] - before[1]) + (up[2] - down[2])
                    div = div + m * (roll(now[3], -1) - roll(now[3], 1))
                    div = ch * div
                    adv = hu * (after[0] - before[0]) + hv * (up[0] - down[0])
                    adv_p = hu * dr_p + hv * dt_p
                    old = [read(base, w, c, l) for c in range(5)]
                    new = [old[0] - adv - div, None, None, None, old[4] - adv_p - heat_ratio * div]
                    push = [None, ch * dr_p, ch * dt_p, cmm * da_p]
                    for c in (1, 2, 3):
                        v = rp * after[c] + rm * before[c] + tp * up[c] + tm * down[c]
                        v = v + ca * (roll(now[c], 2) + roll(now[c], -2)) + cc * now[c]
                        new[c] = old[c] + (v - push[c])
                    if not last:
                        for c in range(5):
                            target[w * 20 + c * 4 + l, here, :] = new[c]
                    elif l % 2 == 0:
                        saved = new
                    else:
                        for c in range(5):
                            both = jnp.where(
                                lane < 64, roll(saved[c], -SIDE), roll(new[c], 64 - SIDE)
                            )
                            out[w, c * 2 + l // 2, pl.ds(t0 - REACH, 8), :] = both
                    before, now = now, after
                return before, now

            first = [read(source, 0, c, 0) for c in range(5)]
            ghost_u = jnp.where(coated, (2.0 * admittance) * first[4], blow) - first[1]
            ghost = [first[0], ghost_u, -first[2], -first[3], first[4]]
            carry = (ghost, first)
            for w in range(8):
                carry = advance(w, carry)
            return 0

        lax.fori_loop(0, (high - low + 7) // 8, chunk, 0)

    h = time_step
    bases = [start, buf_d, start]
    stage = 0
    for step in range(STEPS):
        base = start if step == 0 else buf_d
        plan = [
            (base, buf_b, h / 4.0),
            (buf_b, buf_c, h / 3.0),
            (buf_c, buf_b, h / 2.0),
            (buf_b, buf_d, h),
        ]
        if step == 1:
            plan[3] = (buf_b, buf_c, h)
        if step == 2:
            base = buf_c
            plan = [
                (buf_c, buf_b, h / 4.0),
                (buf_b, buf_d, h / 3.0),
                (buf_d, buf_b, h / 2.0),
                (buf_b, None, h),
            ]
        for source, target, scale in plan:
            stage += 1
            stage_pass(source, base, target, scale, stage, stage == 4 * STEPS)


def unpack_kernel(got, out):
    lane = lane_of((24, 128))
    for q in range(4):
        rows = pl.ds(24 * q, 24)
        for c in range(5):
            for pair in range(2):
                a = got[2 * q, c * 2 + pair]
                b = got[2 * q + 1, c * 2 + pair]
                out[c, 2 * pair, rows, :] = jnp.where(lane < 64, a, roll(b, 64))
                out[c, 2 * pair + 1, rows, :] = jnp.where(lane < 64, roll(a, 64), b)


def shape(*dims):
    return jax.ShapeDtypeStruct(dims, jnp.float32)


def params(mib):
    return pltpu.CompilerParams(vmem_limit_bytes=mib << 20)


def local(state, base_flow, az_scale, blow_table, seg_index, porous):
    place = lax.axis_index("wn")
    quarter, half = place // 2, place % 2
    cells = state.reshape(20, 96, 128)
    walls, head, tail = pl.pallas_call(
        edges_kernel,
        out_shape=(shape(2, 96, 128), shape(6, 96, 128), shape(6, 96, 128)),
        in_specs=[SMEM, VMEM, VMEM, VMEM],
        out_specs=(VMEM, VMEM, VMEM),
        compiler_params=params(24),
        name="edges",
    )(blow_table, cells, seg_index, porous)
    count = lax.axis_size("az")
    before = lax.ppermute(tail, "az", [(i, (i + 1) % count) for i in range(count)])
    after = lax.ppermute(head, "az", [((i + 1) % count, i) for i in range(count)])
    near = jnp.concatenate(
        [cells[:, :REACH], walls[:, :REACH], before[:, :REACH], after[:, :REACH]], 0
    )
    pole = lax.ppermute(
        jnp.flip(near, 1), "az", [(i, (i + count // 2) % count) for i in range(count)]
    )
    def cycles(x, sign):
        return jnp.concatenate(
            [sign * x[..., REACH - 1 :: -1], x, jnp.zeros_like(x[..., :REACH])], -1
        )

    flow = jnp.stack([cycles(base_flow[0], 1.0), cycles(base_flow[1], -1.0)], -1)
    flow = jnp.pad(flow, ((0, 0), (0, 0), (0, 126)))
    pieces, wall_window = pl.pallas_call(
        windows_kernel,
        out_shape=(shape(8, 20, ROWS, 128), shape(2, ROWS, 128)),
        in_specs=[SMEM] + [VMEM] * 6,
        out_specs=(VMEM, VMEM),
        compiler_params=params(32),
        name="windows",
    )(jnp.stack([quarter, half]).astype(jnp.int32), cells, walls, flow, before, after, pole)

    near_axis = lax.dynamic_slice_in_dim(cycles(az_scale, -1.0), OWN_T * quarter, ROWS)
    metric = jnp.broadcast_to(near_axis[:, None], (ROWS, 128))
    cycle = lax.broadcasted_iota(jnp.int32, (ROWS, 128), 0) + (OWN_T * quarter - REACH)
    valid = jnp.where(cycle < 96, 1.0, 0.0).astype(jnp.float32)

    got = lax.all_to_all(pieces, "wn", 0, 0, tiled=True)
    done = pl.pallas_call(
        steps_kernel,
        out_shape=shape(8, 10, OWN_T, 128),
        in_specs=[VMEM] * 4,
        out_specs=VMEM,
        scratch_shapes=[pltpu.VMEM((2, 32, ROWS, 128), jnp.float32)]
        + [pltpu.VMEM((160, ROWS, 128), jnp.float32)] * 3,
        compiler_params=params(48),
        name="steps",
    )(got.reshape(160, ROWS, 128), metric, valid, wall_window)
    back = lax.all_to_all(done, "wn", 0, 0, tiled=True)
    return pl.pallas_call(
        unpack_kernel,
        out_shape=shape(5, 4, 96, 128),
        in_specs=[VMEM],
        out_specs=VMEM,
        compiler_params=params(24),
        name="unpack",
    )(back)


def solution(mesh):
    return jax.shard_map(
        local,
        mesh=mesh,
        in_specs=(
            P(None, "wn", None, "az"),
            P(None, "wn", None),
            P(),
            P(),
            P(None, "az"),
            P(None, "az"),
        ),
        out_specs=P(None, "wn", None, "az"),
        check_vma=False,
    )
```

profile of v0, /device:TPU:2, one launch (start us, length us, event | category | flops | bytes accessed | tf_op | source)
XLA Modules:
  0.0 141.1 jit_solution(9809936619546650430)
XLA Ops:
  0.0 1.2 copy-done
  1.2 0.8 copy-done.3
  2.0 0.8 copy-done.4
  2.8 0.7 copy-done.5
  3.5 1.0 edges.1
  4.6 1.7 %collective-permute-start.1 = (f32[6,96,128]{2,1,0:T(8,128)S(1)}, f32[6,96,128]{2,1,0:T(8,128)S(1)}, u32[]{:S(2)}, u32[]{:S(2)}) collective-permute-start(f32[6,96,128]{2,1,0:T(8,128)S(1)} %get-tuple-element.12), channel_id=1, source_target_pairs={{8,0},{16,8},{24,16},{32,24},{40,32},{48,40},{56,48},{64,56},{72,6... | collective-permute-start | bytes 884744 | tf_op jit(solution)/shard_map/ppermute | solution.py:247
  6.3 0.9 slice.36
  7.2 0.7 slice_bitcast_fusion.1
  7.9 0.1 rev.14
  8.1 0.1 rev.13
  8.1 0.7 rev.16
  8.9 0.7 maximum_maximum_fusion
  9.7 1.0 collective-permute-done.before
  10.8 0.1 rev.15
  10.9 2.0 %collective-permute-start.2 = (f32[34,12,128]{2,1,0:T(8,128)S(1)}, f32[34,12,128]{2,1,0:T(8,128)S(1)}, u32[]{:S(2)}, u32[]{:S(2)}) collective-permute-start(f32[34,12,128]{2,1,0:T(8,128)S(1)} %rev.15), channel_id=1, source_target_pairs={{0,64},{8,72},{16,80},{24,88},{32,96},{40,104},{48,112},{56,120},{... | collective-permute-start | bytes 626696 | tf_op jit(solution)/shard_map/ppermute | solution.py:251
  12.9 0.1 copy.9
  13.1 6.6 %collective-permute-done.2.pole = f32[34,12,128]{2,1,0:T(8,128)S(1)} collective-permute-done((f32[34,12,128]{2,1,0:T(8,128)S(1)}, f32[34,12,128]{2,1,0:T(8,128)S(1)}, u32[]{:S(2)}, u32[]{:S(2)}) %collective-permute-start.2) | collective-permute-done | bytes 208928 | tf_op jit(solution)/shard_map/ppermute | solution.py:251
  19.7 1.8 %windows.1 = (f32[8,20,48,128]{3,2,1,0:T(8,128)S(1)}, f32[2,48,128]{2,1,0:T(8,128)S(1)}) custom-call(s32[2]{0:T(128)S(1)} %pad_add_fusion.place, f32[20,96,128]{2,1,0:T(8,128)S(1)} %bitcast.17, f32[2,96,128]{2,1,0:T(8,128)S(1)} %get-tuple-element.10.walls, f32[4,120,128]{2,1,0:T(8,128)S(1)} %pad.4.flow, f32[6,96,128]{2,1,0:T(8,128)S(1)} %collective-permute-done.before, ...), custom_call_target="tpu_custom_call" | custom-call | tf_op jit(solution)/shard_map/windows/pallas_call | solution.py:261
  21.5 1.9 %copy-done.2 = f32[8,20,48,128]{3,2,1,0:T(8,128)} copy-done((f32[8,20,48,128]{3,2,1,0:T(8,128)}, f32[8,20,48,128]{3,2,1,0:T(8,128)S(1)}, u32[]{:S(2)}) %copy-start.2) | copy-done | bytes 3932184
  23.4 8.0 %all-to-all-start = ((f32[8,20,48,128]{3,2,1,0:T(8,128)}), f32[8,20,48,128]{3,2,1,0:T(8,128)}, u32[]{:S(2)}, u32[]{:S(2)}) async-start(f32[8,20,48,128]{3,2,1,0:T(8,128)} %copy-done.2), calls=%async_computation | async-start | bytes 7864320 | tf_op jit(solution)/shard_map/all_to_all | solution.py:275
  31.5 56.5 %all-to-all-done = f32[8,20,48,128]{3,2,1,0:T(8,128)} async-done(((f32[8,20,48,128]{3,2,1,0:T(8,128)}), f32[8,20,48,128]{3,2,1,0:T(8,128)}, u32[]{:S(2)}, u32[]{:S(2)}) %all-to-all-start) | async-done | bytes 3932192 | tf_op jit(solution)/shard_map/all_to_all | solution.py:275
  88.1 30.9 %steps.1 = f32[8,10,24,128]{3,2,1,0:T(8,128)S(1)} custom-call(f32[160,48,128]{2,1,0:T(8,128)} %bitcast.7.start, f32[48,128]{1,0:T(8,128)S(1)} %broadcast_in_dim.14.metric, f32[48,128]{1,0:T(8,128)S(1)} %iota.7.valid, f32[2,48,128]{2,1,0:T(8,128)S(1)} %get-tuple-element.14.wall), custom_call_target="tpu_custom_call" | custom-call | tf_op jit(solution)/shard_map/steps/pallas_call | solution.py:276
  119.0 20.8 %all_to_all.10.got = f32[8,10,24,128]{3,2,1,0:T(8,128)S(1)} all-to-all(f32[8,10,24,128]{3,2,1,0:T(8,128)S(1)} %steps.1), channel_id=1, replica_groups=mesh['az'=16,'wn'=8] {'wn'}, dimensions={0} | all-to-all | bytes 1966080 | tf_op jit(solution)/shard_map/all_to_all | solution.py:286
  139.8 1.3 unpack.1
  (24 shorter events, 0.5 us)
Async XLA Ops:
  0.0 1.2 copy-start
  1.2 0.8 copy-start.3
  2.0 0.8 copy-start.4
  2.8 0.7 copy-start.5
  3.5 16.3 %copy-start.1 = (f32[5,4,96,128]{3,2,1,0:T(8,128)S(1)}, f32[5,4,96,128]{3,2,1,0:T(8,128)}, u32[]{:S(2)}) copy-start(f32[5,4,96,128]{3,2,1,0:T(8,128)} %param.6) | copy-start | bytes 2949124
  4.5 6.2 %collective-permute-start = (f32[6,96,128]{2,1,0:T(8,128)S(1)}, f32[6,96,128]{2,1,0:T(8,128)S(1)}, u32[]{:S(2)}, u32[]{:S(2)}) collective-permute-start(f32[6,96,128]{2,1,0:T(8,128)S(1)} %get-tuple-element.11), channel_id=1, source_target_pairs={{0,8},{8,16},{16,24},{24,32},{32,40},{40,48},{48,56},{56,64},{64,7... | collective-permute-start | bytes 884744 | tf_op jit(solution)/shard_map/ppermute | solution.py:246
  4.6 6.1 %collective-permute-start.1 = (f32[6,96,128]{2,1,0:T(8,128)S(1)}, f32[6,96,128]{2,1,0:T(8,128)S(1)}, u32[]{:S(2)}, u32[]{:S(2)}) collective-permute-start(f32[6,96,128]{2,1,0:T(8,128)S(1)} %get-tuple-element.12), channel_id=1, source_target_pairs={{8,0},{16,8},{24,16},{32,24},{40,32},{48,40},{56,48},{64,56},{72,6... | collective-permute-start | bytes 884744 | tf_op jit(solution)/shard_map/ppermute | solution.py:247
  10.9 8.9 %collective-permute-start.2 = (f32[34,12,128]{2,1,0:T(8,128)S(1)}, f32[34,12,128]{2,1,0:T(8,128)S(1)}, u32[]{:S(2)}, u32[]{:S(2)}) collective-permute-start(f32[34,12,128]{2,1,0:T(8,128)S(1)} %rev.15), channel_id=1, source_target_pairs={{0,64},{8,72},{16,80},{24,88},{32,96},{40,104},{48,112},{56,120},{... | collective-permute-start | bytes 626696 | tf_op jit(solution)/shard_map/ppermute | solution.py:251
  21.5 1.9 %copy-start.2 = (f32[8,20,48,128]{3,2,1,0:T(8,128)}, f32[8,20,48,128]{3,2,1,0:T(8,128)S(1)}, u32[]{:S(2)}) copy-start(f32[8,20,48,128]{3,2,1,0:T(8,128)S(1)} %get-tuple-element.13) | copy-start | bytes 11796484
  23.4 64.6 %all-to-all-start = ((f32[8,20,48,128]{3,2,1,0:T(8,128)}), f32[8,20,48,128]{3,2,1,0:T(8,128)}, u32[]{:S(2)}, u32[]{:S(2)}) async-start(f32[8,20,48,128]{3,2,1,0:T(8,128)} %copy-done.2), calls=%async_computation | async-start | bytes 7864320 | tf_op jit(solution)/shard_map/all_to_all | solution.py:275
where the time goes:
time: 142 us; the launch traced here: 141 us
  waiting for transfers between devices  64.1 us (45%)
  Pallas kernels  35 us (25%)
  blocking collectives  20.8 us (15%)
  starting transfers between devices  11.8 us (8%)
  local copies, waits for them, and re-layouts  8.36 us (6%)
    all_to_all x1, waiting for transfers between devices, local(): got = lax.all_to_all(pieces, 'wn', 0, 0, tiled=True)  56.5 us
    pallas_call x1, Pallas kernels, local(): pl.pallas_call(steps_kernel, out_shape=shape(8, 10, OWN_T, 128), in_specs...  30.9 us
    all_to_all x1, blocking collectives, local(): back = lax.all_to_all(done, 'wn', 0, 0, tiled=True)  20.8 us
    all_to_all x1, starting transfers between devices, local(): got = lax.all_to_all(pieces, 'wn', 0, 0, tiled=True)  8 us
    ppermute x1, waiting for transfers between devices, local(): lax.ppermute(jnp.flip(near, 1), 'az', [(i, (i + count // 2) % count) for...  6.58 us
    unnamed x12, local copies, waits for them, and re-layouts  5.31 us
  transfers between devices with their start and end apart: 4, of which 3 were waited for; matrix products, arithmetic and copies ran while one was open for 3% of the time, Pallas kernels for 0%

commit v1 on v0

v1 whole, which is shorter than its diff:
```python
import jax
import jax.numpy as jnp
from jax import lax
from jax.experimental import pallas as pl
from jax.experimental.pallas import tpu as pltpu
from jax.sharding import PartitionSpec as P

STEPS = 3
time_step = 0.25
viscosity = 0.05
heat_ratio = 1.4
admittance = 0.6

REACH = 12
OWN_T = 24
ROWS = OWN_T + 2 * REACH
SIDE = 32
FLOW = 10 * ROWS
SIGNS = (1.0, 1.0, -1.0, -1.0, 1.0)
VMEM = pl.BlockSpec(memory_space=pltpu.VMEM)
SMEM = pl.BlockSpec(memory_space=pltpu.SMEM)


def lane_of(shape):
    return lax.broadcasted_iota(jnp.int32, shape, len(shape) - 1)


def roll(x, shift):
    shift = shift % 128
    return pltpu.roll(x, shift, x.ndim - 1) if shift else x


def low_lanes(shape):
    return lane_of(shape) < 64


def inner_lanes(shape):
    return lane_of(shape) % 64 < SIDE


def halves_kernel(core, table, state, seg, porous, keep, send, keep_pole, send_pole):
    first = core[0] == 0
    low = low_lanes((96, 128))

    def split(tile, even, odd, sign):
        left = jnp.where(low, even, roll(odd, 64))
        right = jnp.where(low, roll(even, 64), odd)
        keep[tile] = jnp.where(first, left, right)
        send[tile] = jnp.where(first, right, left)
        for i in range(REACH):
            keep_pole[tile, pl.ds(REACH - 1 - i, 1), :] = sign * keep[tile, pl.ds(i, 1), :]
            send_pole[tile, pl.ds(REACH - 1 - i, 1), :] = sign * send[tile, pl.ds(i, 1), :]

    for c in range(5):
        for i in range(2):
            split(c * 2 + i, state[c * 4 + 2 * i], state[c * 4 + 2 * i + 1], SIGNS[c])
    seg_now = seg[...]
    blowing = jnp.zeros(seg_now.shape, jnp.float32)
    for k in range(16):
        blowing = jnp.where(seg_now == k, table[k], blowing)
    split(10, 2.0 * blowing, porous[...].astype(jnp.float32), 1.0)


def windows_kernel(place, keep, got, keep_pole, got_pole, flow, pieces, wall):
    quarter, deep, flip = place[0], place[1], place[2]

    def window(block, pole, tile, q):
        if q == 0:
            return jnp.concatenate([pole[tile], block[tile, 0:36, :]], 0)
        if q == 3:
            return jnp.concatenate([block[tile, 60:96, :], jnp.zeros((12, 128), jnp.float32)], 0)
        return block[tile, 24 * q - 12 : 24 * q + 36, :]

    for block, pole, spot in ((keep, keep_pole, flip), (got, got_pole, 1 - flip)):
        for q in range(4):
            for tile in range(10):
                pieces[2 * q + spot, tile * ROWS : (tile + 1) * ROWS, :] = window(
                    block, pole, tile, q
                )
            pieces[2 * q + spot, FLOW : FLOW + 8, :] = flow[q]

            @pl.when(jnp.logical_and(quarter == q, deep == spot))
            def _():
                wall[...] = window(block, pole, 10, q)


def edges_kernel(got, wall, head, tail):
    inner = inner_lanes((ROWS, 128))

    def pack(w, _):
        for c in range(5):
            one = got[w, 2 * c * ROWS : (2 * c + 1) * ROWS, :]
            two = got[w, (2 * c + 1) * ROWS : (2 * c + 2) * ROWS, :]
            turned = roll(one, 64)
            head[w * 5 + c] = jnp.where(inner, turned, roll(two, 64 + SIDE))
            tail[w * 5 + c] = jnp.where(inner, roll(two, 64 - SIDE), turned)
        return 0

    lax.fori_loop(0, 8, pack, 0)
    turned = roll(wall[...], 64)
    head[40] = turned
    tail[40] = turned


def steps_kernel(
    got, head, tail, speed, metric, valid, packed_wall, out, start, wall, buf_b, buf_c, buf_d
):
    nu = viscosity
    lane = lane_of((8, 128))

    low = low_lanes((ROWS, 128))
    inner = inner_lanes((ROWS, 128))

    def widen(own, sides):
        return jnp.where(low, own, sides), roll(jnp.where(low, sides, own), 64)

    def spread(w, _):
        for c in range(5):
            right, left = head[w * 5 + c], tail[w * 5 + c]
            one = got[w, 2 * c * ROWS : (2 * c + 1) * ROWS, :]
            two = got[w, (2 * c + 1) * ROWS : (2 * c + 2) * ROWS, :]
            pair = widen(one, jnp.where(inner, right, left))
            pair += widen(two, jnp.where(inner, roll(right, -SIDE), roll(left, SIDE)))
            for l in range(4):
                start[w * 20 + c * 4 + l] = pair[l]
        return 0

    lax.fori_loop(0, 8, spread, 0)
    wall[0], wall[1] = widen(packed_wall[...], jnp.where(inner, head[40], tail[40]))

    def stage_pass(source, base, target, scale, stage, last):
        low, high = stage, ROWS - stage

        def chunk(i, _):
            t0 = jnp.minimum(low + 8 * i, high - 8)
            here = pl.ds(t0, 8)
            m = metric[here, :]
            cm = scale * valid[here, :]
            ch = 0.5 * cm
            c_nu = nu * cm
            ca = (0.25 * c_nu) * (m * m)
            cc = -(4.0 * c_nu + 2.0 * ca)
            cmm = ch * m
            blow = wall[0, here, :]
            coated = wall[1, here, :] > 0.5

            def read(ref, w, c, l, rows=here):
                return ref[w * 20 + c * 4 + l, rows, :]

            def advance(w, carry):
                before, now = carry
                saved = []
                for l in range(4):
                    r = w * 4 + l + 1
                    if r < 32:
                        after = [read(source, r // 4, c, r % 4) for c in range(5)]
                    else:
                        after = [jnp.zeros((8, 128), jnp.float32)] * 5
                    down = [read(source, w, c, l, pl.ds(t0 - 1, 8)) for c in range(5)]
                    up = [read(source, w, c, l, pl.ds(t0 + 1, 8)) for c in range(5)]
                    hu = cm * speed[0, w * 4 + l, here, :]
                    hv = cm * speed[1, w * 4 + l, here, :]
                    rp, rm, tp, tm = c_nu - hu, c_nu + hu, c_nu - hv, c_nu + hv
                    dr_p = after[4] - before[4]
                    dt_p = up[4] - down[4]
                    da_p = roll(now[4], -1) - roll(now[4], 1)
                    div = (after[1] - before[1]) + (up[2] - down[2])
                    div = div + m * (roll(now[3], -1) - roll(now[3], 1))
                    div = ch * div
                    adv = hu * (after[0] - before[0]) + hv * (up[0] - down[0])
                    adv_p = hu * dr_p + hv * dt_p
                    old = [read(base, w, c, l) for c in range(5)]
                    new = [old[0] - adv - div, None, None, None, old[4] - adv_p - heat_ratio * div]
                    push = [None, ch * dr_p, ch * dt_p, cmm * da_p]
                    for c in (1, 2, 3):
                        v = rp * after[c] + rm * before[c] + tp * up[c] + tm * down[c]
                        v = v + ca * (roll(now[c], 2) + roll(now[c], -2)) + cc * now[c]
                        new[c] = old[c] + (v - push[c])
                    if not last:
                        for c in range(5):
                            target[w * 20 + c * 4 + l, here, :] = new[c]
                    elif l % 2 == 0:
                        saved = new
                    else:
                        for c in range(5):
                            both = jnp.where(
                                lane < 64, saved[c], roll(new[c], 64)
                            )
                            out[w, c * 2 + l // 2, pl.ds(t0 - REACH, 8), :] = both
                    before, now = now, after
                return before, now

            first = [read(source, 0, c, 0) for c in range(5)]
            ghost_u = jnp.where(coated, (2.0 * admittance) * first[4], blow) - first[1]
            ghost = [first[0], ghost_u, -first[2], -first[3], first[4]]
            carry = (ghost, first)
            for w in range(8):
                carry = advance(w, carry)
            return 0

        lax.fori_loop(0, (high - low + 7) // 8, chunk, 0)

    h = time_step
    bases = [start, buf_d, start]
    stage = 0
    for step in range(STEPS):
        base = start if step == 0 else buf_d
        plan = [
            (base, buf_b, h / 4.0),
            (buf_b, buf_c, h / 3.0),
            (buf_c, buf_b, h / 2.0),
            (buf_b, buf_d, h),
        ]
        if step == 1:
            plan[3] = (buf_b, buf_c, h)
        if step == 2:
            base = buf_c
            plan = [
                (buf_c, buf_b, h / 4.0),
                (buf_b, buf_d, h / 3.0),
                (buf_d, buf_b, h / 2.0),
                (buf_b, None, h),
            ]
        for source, target, scale in plan:
            stage += 1
            stage_pass(source, base, target, scale, stage, stage == 4 * STEPS)


def join_kernel(place, back, got, out):
    flip, first = place[0], place[1] == 0
    low = low_lanes((OWN_T, 128))
    for q in range(4):
        rows = pl.ds(OWN_T * q, OWN_T)
        for c in range(5):
            for i in range(2):
                mine, other = back[2 * q + flip, c * 2 + i], got[q, c * 2 + i]
                left = jnp.where(first, mine, other)
                right = jnp.where(first, other, mine)
                out[c, 2 * i, rows, :] = jnp.where(low, left, roll(right, 64))
                out[c, 2 * i + 1, rows, :] = jnp.where(low, roll(left, 64), right)


def shape(*dims):
    return jax.ShapeDtypeStruct(dims, jnp.float32)


def params(mib):
    return pltpu.CompilerParams(vmem_limit_bytes=mib << 20)


def right_pairs():
    pairs = []
    for az in range(16):
        for wn in range(8):
            group, core, y, deep = az // 2, az % 2, wn // 2, wn % 2
            strip = 2 * (2 * group + (deep ^ (group % 2))) + core
            strip = (strip + 1) % 32
            group, core = strip // 4, strip % 2
            deep = (strip // 2 % 2) ^ (group % 2)
            pairs.append((az * 8 + wn, (2 * group + core) * 8 + 2 * y + deep))
    return pairs


def local(state, base_flow, az_scale, blow_table, seg_index, porous):
    sector, slab = lax.axis_index("az"), lax.axis_index("wn")
    core, quarter, deep = sector % 2, slab // 2, slab % 2
    flip = (sector // 2 % 2) ^ core
    count = lax.axis_size("az")
    opposite = [(i + count // 2) % count for i in range(count)]

    keep, send, keep_pole, send_pole = pl.pallas_call(
        halves_kernel,
        out_shape=(
            shape(11, 96, 128),
            shape(11, 96, 128),
            shape(11, REACH, 128),
            shape(11, REACH, 128),
        ),
        in_specs=[SMEM, SMEM, VMEM, VMEM, VMEM],
        out_specs=(VMEM,) * 4,
        compiler_params=params(24),
        name="halves",
    )(core[None].astype(jnp.int32), blow_table, state.reshape(20, 96, 128), seg_index, porous)
    swap = [(i, i ^ 1) for i in range(count)]
    keep_pole = lax.ppermute(keep_pole, "az", list(enumerate(opposite)))
    got_pole = lax.ppermute(send_pole, "az", [(i, j ^ 1) for i, j in enumerate(opposite)])
    got = lax.ppermute(send, "az", swap)

    def cycles(x, sign):
        return jnp.concatenate(
            [sign * x[..., REACH - 1 :: -1], x, jnp.zeros_like(x[..., :REACH])], -1
        )

    flow = jnp.concatenate([cycles(base_flow[0], 1.0), cycles(base_flow[1], -1.0)], 0)
    flow = jnp.stack([flow[:, OWN_T * q : OWN_T * q + ROWS] for q in range(4)])
    flow = jnp.pad(0.5 * flow, ((0, 0), (0, 0), (0, 128 - ROWS)))
    near_axis = lax.dynamic_slice_in_dim(cycles(az_scale, -1.0), OWN_T * quarter, ROWS)
    metric = jnp.broadcast_to(near_axis[:, None], (ROWS, 128))
    cycle = lax.broadcasted_iota(jnp.int32, (ROWS, 128), 0) + (OWN_T * quarter - REACH)
    valid = jnp.where(cycle < 96, 1.0, 0.0).astype(jnp.float32)

    pieces, wall = pl.pallas_call(
        windows_kernel,
        out_shape=(shape(8, FLOW + 8, 128), shape(ROWS, 128)),
        in_specs=[SMEM] + [VMEM] * 5,
        out_specs=(VMEM, VMEM),
        compiler_params=params(24),
        name="windows",
    )(
        jnp.stack([quarter, deep, flip]).astype(jnp.int32),
        keep,
        got,
        keep_pole,
        got_pole,
        flow,
    )
    got = lax.all_to_all(pieces, "wn", 0, 0, tiled=True)
    head, tail = pl.pallas_call(
        edges_kernel,
        out_shape=(shape(41, ROWS, 128), shape(41, ROWS, 128)),
        in_specs=[VMEM, VMEM],
        out_specs=(VMEM, VMEM),
        compiler_params=params(24),
        name="edges",
    )(got, wall)
    pairs = right_pairs()
    head = lax.ppermute(head, ("az", "wn"), [(j, i) for i, j in pairs])
    tail = lax.ppermute(tail, ("az", "wn"), pairs)
    speed = got[:, FLOW:, :ROWS].reshape(8, 2, 4, ROWS).transpose(1, 0, 2, 3)
    speed = jnp.broadcast_to(speed.reshape(2, 32, ROWS, 1), (2, 32, ROWS, 128))

    done = pl.pallas_call(
        steps_kernel,
        out_shape=shape(8, 10, OWN_T, 128),
        in_specs=[VMEM] * 7,
        out_specs=VMEM,
        scratch_shapes=[
            pltpu.VMEM((160, ROWS, 128), jnp.float32),
            pltpu.VMEM((2, ROWS, 128), jnp.float32),
        ]
        + [pltpu.VMEM((160, ROWS, 128), jnp.float32)] * 3,
        compiler_params=params(48),
        name="steps",
    )(got, head, tail, speed, metric, valid, wall)
    back = lax.all_to_all(done, "wn", 0, 0, tiled=True)
    other = lax.dynamic_index_in_dim(
        back.reshape(4, 2, 10, OWN_T, 128), 1 - flip, axis=1, keepdims=False
    )
    other = lax.ppermute(other, "az", swap)
    return pl.pallas_call(
        join_kernel,
        out_shape=shape(5, 4, 96, 128),
        in_specs=[SMEM, VMEM, VMEM],
        out_specs=VMEM,
        compiler_params=params(24),
        name="join",
    )(jnp.stack([flip, core]).astype(jnp.int32), back, other)


def solution(mesh):
    return jax.shard_map(
        local,
        mesh=mesh,
        in_specs=(
            P(None, "wn", None, "az"),
            P(None, "wn", None),
            P(),
            P(),
            P(None, "az"),
            P(None, "az"),
        ),
        out_specs=P(None, "wn", None, "az"),
        check_vma=False,
    )
```

time: 142 us -> 133 us (0.937)
  the two profiles are of different devices: /device:TPU:2 before, /device:TPU:1 now
where the time goes in v1:
time: 133 us
  Pallas kernels  39.8 us (30%)
  waiting for transfers between devices  39.1 us (29%)
  blocking collectives  33.2 us (25%)
  starting transfers between devices  14.8 us (11%)
  local copies, waits for them, and re-layouts  5.26 us (4%)
    pallas_call x1, Pallas kernels, local(): pl.pallas_call(steps_kernel, out_shape=shape(8, 10, OWN_T, 128), in_specs...  33.7 us
    all_to_all x1, blocking collectives, local(): got = lax.all_to_all(pieces, 'wn', 0, 0, tiled=True)  33.2 us
    ppermute x1, waiting for transfers between devices, local(): head = lax.ppermute(head, ('az', 'wn'), [(j, i) for i, j in pairs])  12.4 us
    all_to_all x1, waiting for transfers between devices, local(): back = lax.all_to_all(done, 'wn', 0, 0, tiled=True)  11.8 us
    ppermute x1, waiting for transfers between devices, local(): tail = lax.ppermute(tail, ('az', 'wn'), pairs)  9.77 us
    ppermute x1, starting transfers between devices, local(): other = lax.ppermute(other, 'az', swap)  4.68 us
    all_to_all x1, starting transfers between devices, local(): back = lax.all_to_all(done, 'wn', 0, 0, tiled=True)  3.56 us
    unnamed x12, local copies, waits for them, and re-layouts  3.46 us
  transfers between devices with their start and end apart: 7, of which 6 were waited for; matrix products, arithmetic and copies ran while one was open for 1% of the time, Pallas kernels for 0%

profile of v1, /device:TPU:1, one launch (start us, length us, event | category | flops | bytes accessed | tf_op | source)
XLA Modules:
  0.0 132.5 jit_solution(13657100565432941691)
XLA Ops:
  0.0 1.2 copy-done.1
  1.2 0.8 copy-done.2
  2.0 0.8 copy-done.3
  2.8 0.7 copy-done.4
  3.5 0.9 halves.1
  4.4 1.5 %collective-permute-start = (f32[11,96,128]{2,1,0:T(8,128)S(1)}, f32[11,96,128]{2,1,0:T(8,128)S(1)}, u32[]{:S(2)}, u32[]{:S(2)}) collective-permute-start(f32[11,96,128]{2,1,0:T(8,128)S(1)} %get-tuple-element.14), channel_id=1, source_target_pairs={{0,8},{8,0},{16,24},{24,16},{32,40},{40,32},{48,56},{56,48},{64,72... | collective-permute-start | bytes 1622024 | tf_op jit(solution)/shard_map/ppermute | solution.py:287
  5.9 1.7 %collective-permute-start.1 = (f32[11,12,128]{2,1,0:T(8,128)S(1)}, f32[11,12,128]{2,1,0:T(8,128)S(1)}, u32[]{:S(2)}, u32[]{:S(2)}) collective-permute-start(f32[11,12,128]{2,1,0:T(8,128)S(1)} %get-tuple-element.15), channel_id=1, source_target_pairs={{0,64},{8,72},{16,80},{24,88},{32,96},{40,104},{48,112},{56,120},{... | collective-permute-start | bytes 202760 | tf_op jit(solution)/shard_map/ppermute | solution.py:285
  7.7 0.7 slice_bitcast_fusion.5
  8.9 1.6 %collective-permute-done.1.keep_pole = f32[11,12,128]{2,1,0:T(8,128)S(1)} collective-permute-done((f32[11,12,128]{2,1,0:T(8,128)S(1)}, f32[11,12,128]{2,1,0:T(8,128)S(1)}, u32[]{:S(2)}, u32[]{:S(2)}) %collective-permute-start.1) | collective-permute-done | bytes 67616 | tf_op jit(solution)/shard_map/ppermute | solution.py:285
  10.5 2.1 %collective-permute-done.2.got_pole = f32[11,12,128]{2,1,0:T(8,128)S(1)} collective-permute-done((f32[11,12,128]{2,1,0:T(8,128)S(1)}, f32[11,12,128]{2,1,0:T(8,128)S(1)}, u32[]{:S(2)}, u32[]{:S(2)}) %collective-permute-start.2) | collective-permute-done | bytes 67616 | tf_op jit(solution)/shard_map/ppermute | solution.py:286
  12.6 0.7 windows.1
  13.3 33.2 %all_to_all.10.got = f32[8,488,128]{2,1,0:T(8,128)S(1)} all-to-all(f32[8,488,128]{2,1,0:T(8,128)S(1)} %get-tuple-element.17), channel_id=1, replica_groups=mesh['az'=16,'wn'=8] {'wn'}, dimensions={0} | all-to-all | bytes 3997696 | tf_op jit(solution)/shard_map/all_to_all | solution.py:317
  46.5 2.7 %edges.1 = (f32[41,48,128]{2,1,0:T(8,128)}, f32[41,48,128]{2,1,0:T(8,128)}) custom-call(f32[8,488,128]{2,1,0:T(8,128)S(1)} %all_to_all.10.got, f32[48,128]{1,0:T(8,128)S(1)} %get-tuple-element.18.wall.packed_wall), custom_call_target="tpu_custom_call" | custom-call | tf_op jit(solution)/shard_map/edges/pallas_call | solution.py:318
  49.1 1.9 %collective-permute-start.3 = (f32[41,48,128]{2,1,0:T(8,128)}, f32[41,48,128]{2,1,0:T(8,128)S(1)}, u32[]{:S(2)}, u32[]{:S(2)}) collective-permute-start(f32[41,48,128]{2,1,0:T(8,128)} %get-tuple-element.19), channel_id=1, source_target_pairs={{8,0},{9,1},{10,2},{11,3},{12,4},{13,5},{14,6},{15,7},{1,8},{17,9}... | collective-permute-start | bytes 3022856 | tf_op jit(solution)/shard_map/ppermute | solution.py:327
  51.1 1.3 collective-permute-start.4
  52.7 12.4 %collective-permute-done.3.head = f32[41,48,128]{2,1,0:T(8,128)S(1)} collective-permute-done((f32[41,48,128]{2,1,0:T(8,128)}, f32[41,48,128]{2,1,0:T(8,128)S(1)}, u32[]{:S(2)}, u32[]{:S(2)}) %collective-permute-start.3) | collective-permute-done | bytes 1007648 | tf_op jit(solution)/shard_map/ppermute | solution.py:327
  65.0 9.8 %collective-permute-done.4.tail = f32[41,48,128]{2,1,0:T(8,128)} collective-permute-done((f32[41,48,128]{2,1,0:T(8,128)}, f32[41,48,128]{2,1,0:T(8,128)}, u32[]{:S(2)}, u32[]{:S(2)}) %collective-permute-start.4) | collective-permute-done | bytes 1007648 | tf_op jit(solution)/shard_map/ppermute | solution.py:328
  74.8 0.5 broadcast_in_dim.23.speed
  75.4 33.7 %steps.1 = f32[8,10,24,128]{3,2,1,0:T(8,128)} custom-call(f32[8,488,128]{2,1,0:T(8,128)} %copy-done, f32[41,48,128]{2,1,0:T(8,128)S(1)} %collective-permute-done.3.head, f32[41,48,128]{2,1,0:T(8,128)} %collective-permute-done.4.tail, f32[2,32,48,128]{3,2,1,0:T(8,128)S(1)} %broadcast_in_dim.23.speed, f32[48,128]{1,0:T(8,128)S(1)} %broadcast_in_dim.24.metric, ...), custom_call_target="tpu_custom_call" | custom-call | tf_op jit(solution)/shard_map/steps/pallas_call | solution.py:332
  109.1 3.6 %all-to-all-start.1 = ((f32[8,10,24,128]{3,2,1,0:T(8,128)}), f32[8,10,24,128]{3,2,1,0:T(8,128)S(1)}, u32[]{:S(2)}, u32[]{:S(2)}) async-start(f32[8,10,24,128]{3,2,1,0:T(8,128)} %steps.1), calls=%async_computation.1 | async-start | bytes 1966080 | tf_op jit(solution)/shard_map/all_to_all | solution.py:345
  112.6 11.8 %all-to-all-done.1.back = f32[8,10,24,128]{3,2,1,0:T(8,128)S(1)} async-done(((f32[8,10,24,128]{3,2,1,0:T(8,128)}), f32[8,10,24,128]{3,2,1,0:T(8,128)S(1)}, u32[]{:S(2)}, u32[]{:S(2)}) %all-to-all-start.1) | async-done | bytes 983072 | tf_op jit(solution)/shard_map/all_to_all | solution.py:345
  124.5 4.7 %collective-permute-start.5 = (f32[4,10,24,128]{3,2,1,0:T(8,128)S(1)}, f32[4,10,24,128]{3,2,1,0:T(8,128)S(1)}, u32[]{:S(2)}, u32[]{:S(2)}) collective-permute-start(f32[4,10,24,128]{3,2,1,0:T(8,128)S(1)} %dynamic-slice_bitcast_fusion), channel_id=1, source_target_pairs={{0,8},{8,0},{16,24},{24,16},{32,40},{40,32},{48,56},{56,48},{64,72... | collective-permute-start | bytes 1474568 | tf_op jit(solution)/shard_map/ppermute | solution.py:349
  129.3 1.4 %collective-permute-done.5.got = f32[4,10,24,128]{3,2,1,0:T(8,128)S(1)} collective-permute-done((f32[4,10,24,128]{3,2,1,0:T(8,128)S(1)}, f32[4,10,24,128]{3,2,1,0:T(8,128)S(1)}, u32[]{:S(2)}, u32[]{:S(2)}) %collective-permute-start.5) | collective-permute-done | bytes 491552 | tf_op jit(solution)/shard_map/ppermute | solution.py:349
  130.7 1.8 %join.1 = f32[5,4,96,128]{3,2,1,0:T(8,128)} custom-call(s32[2]{0:T(128)S(1)} %pad_add_fusion.place, f32[8,10,24,128]{3,2,1,0:T(8,128)S(1)} %all-to-all-done.1.back, f32[4,10,24,128]{3,2,1,0:T(8,128)S(1)} %collective-permute-done.5.got), custom_call_target="tpu_custom_call" | custom-call | tf_op jit(solution)/shard_map/join/pallas_call | solution.py:350
  (31 shorter events, 1.0 us)
Async XLA Ops:
  0.0 1.2 copy-start.1
  1.2 0.8 copy-start.2
  2.0 0.8 copy-start.3
  2.8 0.7 copy-start.4
  4.4 8.2 %collective-permute-start = (f32[11,96,128]{2,1,0:T(8,128)S(1)}, f32[11,96,128]{2,1,0:T(8,128)S(1)}, u32[]{:S(2)}, u32[]{:S(2)}) collective-permute-start(f32[11,96,128]{2,1,0:T(8,128)S(1)} %get-tuple-element.14), channel_id=1, source_target_pairs={{0,8},{8,0},{16,24},{24,16},{32,40},{40,32},{48,56},{56,48},{64,72... | collective-permute-start | bytes 1622024 | tf_op jit(solution)/shard_map/ppermute | solution.py:287
  5.9 4.6 %collective-permute-start.1 = (f32[11,12,128]{2,1,0:T(8,128)S(1)}, f32[11,12,128]{2,1,0:T(8,128)S(1)}, u32[]{:S(2)}, u32[]{:S(2)}) collective-permute-start(f32[11,12,128]{2,1,0:T(8,128)S(1)} %get-tuple-element.15), channel_id=1, source_target_pairs={{0,64},{8,72},{16,80},{24,88},{32,96},{40,104},{48,112},{56,120},{... | collective-permute-start | bytes 202760 | tf_op jit(solution)/shard_map/ppermute | solution.py:285
  7.6 4.9 %collective-permute-start.2 = (f32[11,12,128]{2,1,0:T(8,128)S(1)}, f32[11,12,128]{2,1,0:T(8,128)S(1)}, u32[]{:S(2)}, u32[]{:S(2)}) collective-permute-start(f32[11,12,128]{2,1,0:T(8,128)S(1)} %get-tuple-element.16), channel_id=1, source_target_pairs={{0,72},{8,64},{16,88},{24,80},{32,104},{40,96},{48,120},{56,112},{... | collective-permute-start | bytes 202760 | tf_op jit(solution)/shard_map/ppermute | solution.py:286
  46.5 28.9 %copy-start = (f32[8,488,128]{2,1,0:T(8,128)}, f32[8,488,128]{2,1,0:T(8,128)S(1)}, u32[]{:S(2)}) copy-start(f32[8,488,128]{2,1,0:T(8,128)S(1)} %all_to_all.10.got) | copy-start | bytes 5996548
  46.5 5.9 %copy-start.5 = (f32[96]{0:T(128)S(1)}, f32[96]{0:T(128)}, u32[]{:S(2)}) copy-start(f32[96]{0:T(128)} %param.8) | copy-start | bytes 1156
  49.1 15.9 %collective-permute-start.3 = (f32[41,48,128]{2,1,0:T(8,128)}, f32[41,48,128]{2,1,0:T(8,128)S(1)}, u32[]{:S(2)}, u32[]{:S(2)}) collective-permute-start(f32[41,48,128]{2,1,0:T(8,128)} %get-tuple-element.19), channel_id=1, source_target_pairs={{8,0},{9,1},{10,2},{11,3},{12,4},{13,5},{14,6},{15,7},{1,8},{17,9}... | collective-permute-start | bytes 3022856 | tf_op jit(solution)/shard_map/ppermute | solution.py:327
  51.1 23.7 %collective-permute-start.4 = (f32[41,48,128]{2,1,0:T(8,128)}, f32[41,48,128]{2,1,0:T(8,128)}, u32[]{:S(2)}, u32[]{:S(2)}) collective-permute-start(f32[41,48,128]{2,1,0:T(8,128)} %get-tuple-element.20), channel_id=1, source_target_pairs={{0,8},{1,9},{2,10},{3,11},{4,12},{5,13},{6,14},{7,15},{8,1},{9,17}... | collective-permute-start | bytes 3022856 | tf_op jit(solution)/shard_map/ppermute | solution.py:328
  109.1 15.4 %all-to-all-start.1 = ((f32[8,10,24,128]{3,2,1,0:T(8,128)}), f32[8,10,24,128]{3,2,1,0:T(8,128)S(1)}, u32[]{:S(2)}, u32[]{:S(2)}) async-start(f32[8,10,24,128]{3,2,1,0:T(8,128)} %steps.1), calls=%async_computation.1 | async-start | bytes 1966080 | tf_op jit(solution)/shard_map/all_to_all | solution.py:345
  124.5 6.2 %collective-permute-start.5 = (f32[4,10,24,128]{3,2,1,0:T(8,128)S(1)}, f32[4,10,24,128]{3,2,1,0:T(8,128)S(1)}, u32[]{:S(2)}, u32[]{:S(2)}) collective-permute-start(f32[4,10,24,128]{3,2,1,0:T(8,128)S(1)} %dynamic-slice_bitcast_fusion), channel_id=1, source_target_pairs={{0,8},{8,0},{16,24},{24,16},{32,40},{40,32},{48,56},{56,48},{64,72... | collective-permute-start | bytes 1474568 | tf_op jit(solution)/shard_map/ppermute | solution.py:349

commit v2 on v1

--- a/solution.py
+++ b/solution.py
@@ -18,6 +18,7 @@
 FLOW = 10 * ROWS
 SIGNS = (1.0, 1.0, -1.0, -1.0, 1.0)
 VMEM = pl.BlockSpec(memory_space=pltpu.VMEM)
+HBM = pl.BlockSpec(memory_space=pltpu.HBM)
 SMEM = pl.BlockSpec(memory_space=pltpu.SMEM)
 
 
@@ -38,7 +39,30 @@
     return lane_of(shape) % 64 < SIDE
 
 
-def halves_kernel(core, table, state, seg, porous, keep, send, keep_pole, send_pole):
+def halves_kernel(
+    core,
+    table,
+    state_far,
+    seg_far,
+    porous_far,
+    keep,
+    send,
+    keep_pole,
+    send_pole,
+    state,
+    seg,
+    porous,
+    sems,
+):
+    fetches = [
+        pltpu.make_async_copy(state_far, state, sems.at[0]),
+        pltpu.make_async_copy(seg_far, seg, sems.at[1]),
+        pltpu.make_async_copy(porous_far, porous, sems.at[2]),
+    ]
+    for fetch in fetches:
+        fetch.start()
+    for fetch in fetches:
+        fetch.wait()
     first = core[0] == 0
     low = low_lanes((96, 128))
 
@@ -62,7 +86,7 @@
 
 
 def windows_kernel(place, keep, got, keep_pole, got_pole, flow, pieces, wall):
-    quarter, deep, flip = place[0], place[1], place[2]
+    quarter, odd, flip = place[0], place[1], place[2]
 
     def window(block, pole, tile, q):
         if q == 0:
@@ -74,12 +98,12 @@
     for block, pole, spot in ((keep, keep_pole, flip), (got, got_pole, 1 - flip)):
         for q in range(4):
             for tile in range(10):
-                pieces[2 * q + spot, tile * ROWS : (tile + 1) * ROWS, :] = window(
+                pieces[4 * (q // 2) + 2 * spot + q % 2, tile * ROWS : (tile + 1) * ROWS, :] = window(
                     block, pole, tile, q
                 )
-            pieces[2 * q + spot, FLOW : FLOW + 8, :] = flow[q]
-
-            @pl.when(jnp.logical_and(quarter == q, deep == spot))
+            pieces[4 * (q // 2) + 2 * spot + q % 2, FLOW : FLOW + 8, :] = flow[q]
+
+            @pl.when(jnp.logical_and(quarter == q, odd == spot))
             def _():
                 wall[...] = window(block, pole, 10, q)
 
@@ -88,45 +112,88 @@
     inner = inner_lanes((ROWS, 128))
 
     def pack(w, _):
+        for c in range(1, 5):
+            one = got[w, 2 * c * ROWS : (2 * c + 1) * ROWS, :]
+            two = got[w, (2 * c + 1) * ROWS : (2 * c + 2) * ROWS, :]
+            turned = roll(one, 64)
+            head[w * 4 + c - 1] = jnp.where(inner, turned, roll(two, 64 + SIDE))
+            tail[w * 4 + c - 1] = jnp.where(inner, roll(two, 64 - SIDE), turned)
+        return 0
+
+    lax.fori_loop(0, 8, pack, 0)
+    turned = roll(wall[...], 64)
+    head[32] = turned
+    tail[32] = turned
+
+
+def steps_kernel(
+    got_far,
+    head_far,
+    tail_far,
+    speed_far,
+    metric,
+    valid,
+    packed_wall,
+    out,
+    got,
+    head,
+    tail,
+    speed,
+    start,
+    wall,
+    buf_b,
+    buf_c,
+    buf_d,
+    sems,
+):
+    nu = viscosity
+    lane = lane_of((8, 128))
+
+    low = low_lanes((ROWS, 128))
+    inner = inner_lanes((ROWS, 128))
+
+    def widen(own, sides):
+        return jnp.where(low, own, sides), roll(jnp.where(low, sides, own), 64)
+
+    def fetches(w):
+        part = pl.ds(w * 4, 4)
+        return (
+            pltpu.make_async_copy(got_far.at[w], got.at[w], sems.at[w, 0]),
+            pltpu.make_async_copy(head_far.at[part], head.at[part], sems.at[w, 1]),
+            pltpu.make_async_copy(tail_far.at[part], tail.at[part], sems.at[w, 2]),
+        )
+
+    ends = (
+        pltpu.make_async_copy(head_far.at[32], head.at[32], sems.at[8, 0]),
+        pltpu.make_async_copy(tail_far.at[32], tail.at[32], sems.at[8, 1]),
+        pltpu.make_async_copy(speed_far, speed, sems.at[8, 2]),
+    )
+    for w in range(8):
+        for fetch in fetches(w):
+            fetch.start()
+    for fetch in ends:
+        fetch.start()
+
+    def spread(w, _):
+        for fetch in fetches(w):
+            fetch.wait()
         for c in range(5):
             one = got[w, 2 * c * ROWS : (2 * c + 1) * ROWS, :]
             two = got[w, (2 * c + 1) * ROWS : (2 * c + 2) * ROWS, :]
-            turned = roll(one, 64)
-            head[w * 5 + c] = jnp.where(inner, turned, roll(two, 64 + SIDE))
-            tail[w * 5 + c] = jnp.where(inner, roll(two, 64 - SIDE), turned)
-        return 0
-
-    lax.fori_loop(0, 8, pack, 0)
-    turned = roll(wall[...], 64)
-    head[40] = turned
-    tail[40] = turned
-
-
-def steps_kernel(
-    got, head, tail, speed, metric, valid, packed_wall, out, start, wall, buf_b, buf_c, buf_d
-):
-    nu = viscosity
-    lane = lane_of((8, 128))
-
-    low = low_lanes((ROWS, 128))
-    inner = inner_lanes((ROWS, 128))
-
-    def widen(own, sides):
-        return jnp.where(low, own, sides), roll(jnp.where(low, sides, own), 64)
-
-    def spread(w, _):
-        for c in range(5):
-            right, left = head[w * 5 + c], tail[w * 5 + c]
-            one = got[w, 2 * c * ROWS : (2 * c + 1) * ROWS, :]
-            two = got[w, (2 * c + 1) * ROWS : (2 * c + 2) * ROWS, :]
-            pair = widen(one, jnp.where(inner, right, left))
-            pair += widen(two, jnp.where(inner, roll(right, -SIDE), roll(left, SIDE)))
+            if c:
+                right, left = head[w * 4 + c - 1], tail[w * 4 + c - 1]
+                pair = widen(one, jnp.where(inner, right, left))
+                pair += widen(two, jnp.where(inner, roll(right, -SIDE), roll(left, SIDE)))
+            else:
+                pair = (one, roll(one, 64), two, roll(two, 64))
             for l in range(4):
                 start[w * 20 + c * 4 + l] = pair[l]
         return 0
 
     lax.fori_loop(0, 8, spread, 0)
-    wall[0], wall[1] = widen(packed_wall[...], jnp.where(inner, head[40], tail[40]))
+    for fetch in ends:
+        fetch.wait()
+    wall[0], wall[1] = widen(packed_wall[...], jnp.where(inner, head[32], tail[32]))
 
     def stage_pass(source, base, target, scale, stage, last):
         low, high = stage, ROWS - stage
@@ -198,7 +265,7 @@
                 carry = advance(w, carry)
             return 0
 
-        lax.fori_loop(0, (high - low + 7) // 8, chunk, 0)
+        lax.fori_loop(0, (high - low + 7) // 8, chunk, 0, unroll=2)
 
     h = time_step
     bases = [start, buf_d, start]
@@ -233,7 +300,7 @@
         rows = pl.ds(OWN_T * q, OWN_T)
         for c in range(5):
             for i in range(2):
-                mine, other = back[2 * q + flip, c * 2 + i], got[q, c * 2 + i]
+                mine, other = back[4 * (q // 2) + 2 * flip + q % 2, c * 2 + i], got[q, c * 2 + i]
                 left = jnp.where(first, mine, other)
                 right = jnp.where(first, other, mine)
                 out[c, 2 * i, rows, :] = jnp.where(low, left, roll(right, 64))
@@ -252,18 +319,18 @@
     pairs = []
     for az in range(16):
         for wn in range(8):
-            group, core, y, deep = az // 2, az % 2, wn // 2, wn % 2
-            strip = 2 * (2 * group + (deep ^ (group % 2))) + core
+            group, core, odd = az // 2, az % 2, wn // 2 % 2
+            strip = 2 * (2 * group + (odd ^ (group % 2))) + core
             strip = (strip + 1) % 32
             group, core = strip // 4, strip % 2
-            deep = (strip // 2 % 2) ^ (group % 2)
-            pairs.append((az * 8 + wn, (2 * group + core) * 8 + 2 * y + deep))
+            other = wn + 2 * (((strip // 2 % 2) ^ (group % 2)) - odd)
+            pairs.append((az * 8 + wn, (2 * group + core) * 8 + other))
     return pairs
 
 
 def local(state, base_flow, az_scale, blow_table, seg_index, porous):
     sector, slab = lax.axis_index("az"), lax.axis_index("wn")
-    core, quarter, deep = sector % 2, slab // 2, slab % 2
+    core, quarter, odd = sector % 2, slab // 4 * 2 + slab % 2, slab // 2 % 2
     flip = (sector // 2 % 2) ^ core
     count = lax.axis_size("az")
     opposite = [(i + count // 2) % count for i in range(count)]
@@ -276,8 +343,14 @@
             shape(11, REACH, 128),
             shape(11, REACH, 128),
         ),
-        in_specs=[SMEM, SMEM, VMEM, VMEM, VMEM],
+        in_specs=[SMEM, SMEM, HBM, HBM, HBM],
         out_specs=(VMEM,) * 4,
+        scratch_shapes=[
+            pltpu.VMEM((20, 96, 128), jnp.float32),
+            pltpu.VMEM((96, 128), jnp.int32),
+            pltpu.VMEM((96, 128), jnp.int32),
+            pltpu.SemaphoreType.DMA((3,)),
+        ],
         compiler_params=params(24),
         name="halves",
     )(core[None].astype(jnp.int32), blow_table, state.reshape(20, 96, 128), seg_index, porous)
@@ -307,7 +380,7 @@
         compiler_params=params(24),
         name="windows",
     )(
-        jnp.stack([quarter, deep, flip]).astype(jnp.int32),
+        jnp.stack([quarter, odd, flip]).astype(jnp.int32),
         keep,
         got,
         keep_pole,
@@ -317,7 +390,7 @@
     got = lax.all_to_all(pieces, "wn", 0, 0, tiled=True)
     head, tail = pl.pallas_call(
         edges_kernel,
-        out_shape=(shape(41, ROWS, 128), shape(41, ROWS, 128)),
+        out_shape=(shape(33, ROWS, 128), shape(33, ROWS, 128)),
         in_specs=[VMEM, VMEM],
         out_specs=(VMEM, VMEM),
         compiler_params=params(24),
@@ -332,20 +405,25 @@
     done = pl.pallas_call(
         steps_kernel,
         out_shape=shape(8, 10, OWN_T, 128),
-        in_specs=[VMEM] * 7,
+        in_specs=[HBM] * 4 + [VMEM] * 3,
         out_specs=VMEM,
         scratch_shapes=[
+            pltpu.VMEM((8, FLOW + 8, 128), jnp.float32),
+            pltpu.VMEM((33, ROWS, 128), jnp.float32),
+            pltpu.VMEM((33, ROWS, 128), jnp.float32),
+            pltpu.VMEM((2, 32, ROWS, 128), jnp.float32),
             pltpu.VMEM((160, ROWS, 128), jnp.float32),
             pltpu.VMEM((2, ROWS, 128), jnp.float32),
         ]
-        + [pltpu.VMEM((160, ROWS, 128), jnp.float32)] * 3,
+        + [pltpu.VMEM((160, ROWS, 128), jnp.float32)] * 3
+        + [pltpu.SemaphoreType.DMA((9, 3))],
         compiler_params=params(48),
         name="steps",
     )(got, head, tail, speed, metric, valid, wall)
     back = lax.all_to_all(done, "wn", 0, 0, tiled=True)
     other = lax.dynamic_index_in_dim(
-        back.reshape(4, 2, 10, OWN_T, 128), 1 - flip, axis=1, keepdims=False
-    )
+        back.reshape(2, 2, 2, 10, OWN_T, 128), 1 - flip, axis=1, keepdims=False
+    ).reshape(4, 10, OWN_T, 128)
     other = lax.ppermute(other, "az", swap)
     return pl.pallas_call(
         join_kernel,

time: 133 us -> 118 us (0.89)
  waiting for transfers between devices: 39.1 us -> 25.2 us
  Pallas kernels: 39.8 us -> 37.2 us
    ppermute x1, waiting for transfers between devices: 9.77 us -> 0.01 us  [local(): tail = lax.ppermute(tail, ('az', 'wn'), pairs)]
    pallas_call x1, Pallas kernels: 33.7 us -> 30.9 us  [local(): pl.pallas_call(steps_kernel, out_shape=shape(8, 10, OWN_T, 128), in_specs...]
    ppermute x1, waiting for transfers between devices: 12.4 us -> 10.3 us  [local(): head = lax.ppermute(head, ('az', 'wn'), [(j, i) for i, j in pairs])]
    ppermute x1, starting transfers between devices: 4.68 us -> 6.29 us  [local(): other = lax.ppermute(other, 'az', swap)]
    ppermute x1, waiting for transfers between devices: 1.65 us -> 0.19 us  [local(): keep_pole = lax.ppermute(keep_pole, 'az', list(enumerate(opposite)))]
  transfers between devices with their start and end apart: 7 -> 7, of which waited for: 6 -> 5; matrix products, arithmetic and copies ran while one was open for 1% -> 1% of each run, Pallas kernels for 0% -> 0%
where the time goes in v2:
time: 118 us; the launch traced here: 117 us
  Pallas kernels  37.2 us (32%)
  blocking collectives  33.3 us (28%)
  waiting for transfers between devices  25.2 us (21%)
  starting transfers between devices  16 us (14%)
  local copies, waits for them, and re-layouts  5.26 us (4%)
    all_to_all x1, blocking collectives, local(): got = lax.all_to_all(pieces, 'wn', 0, 0, tiled=True)  33.3 us
    pallas_call x1, Pallas kernels, local(): pl.pallas_call(steps_kernel, out_shape=shape(8, 10, OWN_T, 128), in_specs...  30.9 us
    all_to_all x1, waiting for transfers between devices, local(): back = lax.all_to_all(done, 'wn', 0, 0, tiled=True)  10.7 us
    ppermute x1, waiting for transfers between devices, local(): head = lax.ppermute(head, ('az', 'wn'), [(j, i) for i, j in pairs])  10.3 us
    ppermute x1, starting transfers between devices, local(): other = lax.ppermute(other, 'az', swap)  6.29 us
    all_to_all x1, starting transfers between devices, local(): back = lax.all_to_all(done, 'wn', 0, 0, tiled=True)  3.73 us
    unnamed x12, local copies, waits for them, and re-layouts  3.46 us
    ppermute x1, waiting for transfers between devices, local(): lax.ppermute(send_pole, 'az', [(i, j ^ 1) for i, j in enumerate(opposite)])  2.62 us
  transfers between devices with their start and end apart: 7, of which 5 were waited for; matrix products, arithmetic and copies ran while one was open for 1% of the time, Pallas kernels for 0%

profile of v2, /device:TPU:1, one launch (start us, length us, event | category | flops | bytes accessed | tf_op | source)
XLA Modules:
  0.0 117.3 jit_solution(8135259843442682814)
XLA Ops:
  0.0 1.2 %copy-done.1 = f32[5,4,96,128]{3,2,1,0:T(8,128)S(1)} copy-done((f32[5,4,96,128]{3,2,1,0:T(8,128)S(1)}, f32[5,4,96,128]{3,2,1,0:T(8,128)}, u32[]{:S(2)}) %copy-start.1) | copy-done | bytes 983064
  1.2 0.8 copy-done.2
  2.0 0.8 copy-done.3
  2.8 0.7 copy-done.4
  3.5 1.4 %halves.1 = (f32[11,96,128]{2,1,0:T(8,128)S(1)}, f32[11,96,128]{2,1,0:T(8,128)S(1)}, f32[11,12,128]{2,1,0:T(8,128)S(1)}, f32[11,12,128]{2,1,0:T(8,128)S(1)}) custom-call(s32[1]{0:T(128)} %bitcast.1.core, f32[16]{0:T(128)S(1)} %copy-done.4, f32[20,96,128]{2,1,0:T(8,128)S(1)} %bitcast.29, s32[96,128]{1,0:T(8,128)S(1)} %copy-done.2, s32[96,128]{1,0:T(8,128)S(1)} %copy-done.3), custom_call_target="tpu_custom_call" | custom-call | tf_op jit(solution)/shard_map/halves/pallas_call | solution.py:338
  4.9 2.5 %collective-permute-start.1 = (f32[11,12,128]{2,1,0:T(8,128)S(1)}, f32[11,12,128]{2,1,0:T(8,128)S(1)}, u32[]{:S(2)}, u32[]{:S(2)}) collective-permute-start(f32[11,12,128]{2,1,0:T(8,128)S(1)} %get-tuple-element.15), channel_id=1, source_target_pairs={{0,64},{8,72},{16,80},{24,88},{32,96},{40,104},{48,112},{56,120},{... | collective-permute-start | bytes 202760 | tf_op jit(solution)/shard_map/ppermute | solution.py:358
  7.4 0.7 collective-permute-start.2
  8.1 0.3 collective-permute-start
  8.4 0.7 slice_bitcast_fusion.5
  9.5 0.2 collective-permute-done.1.keep_pole
  9.7 2.6 %collective-permute-done.2.got_pole = f32[11,12,128]{2,1,0:T(8,128)S(1)} collective-permute-done((f32[11,12,128]{2,1,0:T(8,128)S(1)}, f32[11,12,128]{2,1,0:T(8,128)S(1)}, u32[]{:S(2)}, u32[]{:S(2)}) %collective-permute-start.2) | collective-permute-done | bytes 67616 | tf_op jit(solution)/shard_map/ppermute | solution.py:359
  12.3 0.7 windows.1
  13.0 33.3 %all_to_all.10.got.got_far = f32[8,488,128]{2,1,0:T(8,128)S(1)} all-to-all(f32[8,488,128]{2,1,0:T(8,128)S(1)} %get-tuple-element.17), channel_id=1, replica_groups=mesh['az'=16,'wn'=8] {'wn'}, dimensions={0} | all-to-all | bytes 3997696 | tf_op jit(solution)/shard_map/all_to_all | solution.py:390
  46.3 2.3 %edges.1 = (f32[33,48,128]{2,1,0:T(8,128)}, f32[33,48,128]{2,1,0:T(8,128)}) custom-call(f32[8,488,128]{2,1,0:T(8,128)S(1)} %all_to_all.10.got.got_far, f32[48,128]{1,0:T(8,128)S(1)} %get-tuple-element.18.wall.packed_wall), custom_call_target="tpu_custom_call" | custom-call | tf_op jit(solution)/shard_map/edges/pallas_call | solution.py:391
  48.6 2.3 %collective-permute-start.3 = (f32[33,48,128]{2,1,0:T(8,128)}, f32[33,48,128]{2,1,0:T(8,128)S(1)}, u32[]{:S(2)}, u32[]{:S(2)}) collective-permute-start(f32[33,48,128]{2,1,0:T(8,128)} %get-tuple-element.19), channel_id=1, source_target_pairs={{8,0},{9,1},{10,2},{11,3},{12,4},{13,5},{14,6},{15,7},{2,8},{3,9},... | collective-permute-start | bytes 2433032 | tf_op jit(solution)/shard_map/ppermute | solution.py:400
  51.0 0.2 collective-permute-start.4
  51.5 10.3 %collective-permute-done.3.head_far = f32[33,48,128]{2,1,0:T(8,128)S(1)} collective-permute-done((f32[33,48,128]{2,1,0:T(8,128)}, f32[33,48,128]{2,1,0:T(8,128)S(1)}, u32[]{:S(2)}, u32[]{:S(2)}) %collective-permute-start.3) | collective-permute-done | bytes 811040 | tf_op jit(solution)/shard_map/ppermute | solution.py:400
  61.9 0.5 broadcast_in_dim.23.speed_far
  62.3 30.9 %steps.1 = f32[8,10,24,128]{3,2,1,0:T(8,128)} custom-call(f32[8,488,128]{2,1,0:T(8,128)} %copy-done, f32[33,48,128]{2,1,0:T(8,128)S(1)} %collective-permute-done.3.head_far, f32[33,48,128]{2,1,0:T(8,128)} %collective-permute-done.4.tail_far, f32[2,32,48,128]{3,2,1,0:T(8,128)S(1)} %broadcast_in_dim.23.speed_far, f32[48,128]{1,0:T(8,128)S(1)} %broadcast_in_dim.24.metric, ...), custom_call_target="tpu_custom_call" | custom-call | tf_op jit(solution)/shard_map/steps/pallas_call | solution.py:405
  93.3 3.7 %all-to-all-start.1 = ((f32[8,10,24,128]{3,2,1,0:T(8,128)}), f32[8,10,24,128]{3,2,1,0:T(8,128)S(1)}, u32[]{:S(2)}, u32[]{:S(2)}) async-start(f32[8,10,24,128]{3,2,1,0:T(8,128)} %steps.1), calls=%async_computation.1 | async-start | bytes 1966080 | tf_op jit(solution)/shard_map/all_to_all | solution.py:423
  97.0 10.7 %all-to-all-done.1.back = f32[8,10,24,128]{3,2,1,0:T(8,128)S(1)} async-done(((f32[8,10,24,128]{3,2,1,0:T(8,128)}), f32[8,10,24,128]{3,2,1,0:T(8,128)S(1)}, u32[]{:S(2)}, u32[]{:S(2)}) %all-to-all-start.1) | async-done | bytes 983072 | tf_op jit(solution)/shard_map/all_to_all | solution.py:423
  107.7 6.3 %collective-permute-start.5 = (f32[4,10,24,128]{3,2,1,0:T(8,128)S(1)}, f32[4,10,24,128]{3,2,1,0:T(8,128)S(1)}, u32[]{:S(2)}, u32[]{:S(2)}) collective-permute-start(f32[4,10,24,128]{3,2,1,0:T(8,128)S(1)} %bitcast.30), channel_id=1, source_target_pairs={{0,8},{8,0},{16,24},{24,16},{32,40},{40,32},{48,56},{56,48},{64,72... | collective-permute-start | bytes 1474568 | tf_op jit(solution)/shard_map/ppermute | solution.py:427
  114.1 1.4 %collective-permute-done.5.got = f32[4,10,24,128]{3,2,1,0:T(8,128)S(1)} collective-permute-done((f32[4,10,24,128]{3,2,1,0:T(8,128)S(1)}, f32[4,10,24,128]{3,2,1,0:T(8,128)S(1)}, u32[]{:S(2)}, u32[]{:S(2)}) %collective-permute-start.5) | collective-permute-done | bytes 491552 | tf_op jit(solution)/shard_map/ppermute | solution.py:427
  115.5 1.8 %join.1 = f32[5,4,96,128]{3,2,1,0:T(8,128)} custom-call(s32[2]{0:T(128)S(1)} %pad_add_fusion.place, f32[8,10,24,128]{3,2,1,0:T(8,128)S(1)} %all-to-all-done.1.back, f32[4,10,24,128]{3,2,1,0:T(8,128)S(1)} %collective-permute-done.5.got), custom_call_target="tpu_custom_call" | custom-call | tf_op jit(solution)/shard_map/join/pallas_call | solution.py:428
  (31 shorter events, 1.0 us)
Async XLA Ops:
  0.0 1.2 %copy-start.1 = (f32[5,4,96,128]{3,2,1,0:T(8,128)S(1)}, f32[5,4,96,128]{3,2,1,0:T(8,128)}, u32[]{:S(2)}) copy-start(f32[5,4,96,128]{3,2,1,0:T(8,128)} %param.6) | copy-start | bytes 2949124
  1.2 0.8 copy-start.2
  2.0 0.8 copy-start.3
  2.8 0.7 copy-start.4
  4.9 4.9 %collective-permute-start.1 = (f32[11,12,128]{2,1,0:T(8,128)S(1)}, f32[11,12,128]{2,1,0:T(8,128)S(1)}, u32[]{:S(2)}, u32[]{:S(2)}) collective-permute-start(f32[11,12,128]{2,1,0:T(8,128)S(1)} %get-tuple-element.15), channel_id=1, source_target_pairs={{0,64},{8,72},{16,80},{24,88},{32,96},{40,104},{48,112},{56,120},{... | collective-permute-start | bytes 202760 | tf_op jit(solution)/shard_map/ppermute | solution.py:358
  7.4 4.9 %collective-permute-start.2 = (f32[11,12,128]{2,1,0:T(8,128)S(1)}, f32[11,12,128]{2,1,0:T(8,128)S(1)}, u32[]{:S(2)}, u32[]{:S(2)}) collective-permute-start(f32[11,12,128]{2,1,0:T(8,128)S(1)} %get-tuple-element.16), channel_id=1, source_target_pairs={{0,72},{8,64},{16,88},{24,80},{32,104},{40,96},{48,120},{56,112},{... | collective-permute-start | bytes 202760 | tf_op jit(solution)/shard_map/ppermute | solution.py:359
  8.1 4.3 %collective-permute-start = (f32[11,96,128]{2,1,0:T(8,128)S(1)}, f32[11,96,128]{2,1,0:T(8,128)S(1)}, u32[]{:S(2)}, u32[]{:S(2)}) collective-permute-start(f32[11,96,128]{2,1,0:T(8,128)S(1)} %get-tuple-element.14), channel_id=1, source_target_pairs={{0,8},{8,0},{16,24},{24,16},{32,40},{40,32},{48,56},{56,48},{64,72... | collective-permute-start | bytes 1622024 | tf_op jit(solution)/shard_map/ppermute | solution.py:360
  46.3 16.0 %copy-start = (f32[8,488,128]{2,1,0:T(8,128)}, f32[8,488,128]{2,1,0:T(8,128)S(1)}, u32[]{:S(2)}) copy-start(f32[8,488,128]{2,1,0:T(8,128)S(1)} %all_to_all.10.got.got_far) | copy-start | bytes 5996548
  46.3 4.9 %copy-start.5 = (f32[96]{0:T(128)S(1)}, f32[96]{0:T(128)}, u32[]{:S(2)}) copy-start(f32[96]{0:T(128)} %param.8) | copy-start | bytes 1156
  48.6 13.1 %collective-permute-start.3 = (f32[33,48,128]{2,1,0:T(8,128)}, f32[33,48,128]{2,1,0:T(8,128)S(1)}, u32[]{:S(2)}, u32[]{:S(2)}) collective-permute-start(f32[33,48,128]{2,1,0:T(8,128)} %get-tuple-element.19), channel_id=1, source_target_pairs={{8,0},{9,1},{10,2},{11,3},{12,4},{13,5},{14,6},{15,7},{2,8},{3,9},... | collective-permute-start | bytes 2433032 | tf_op jit(solution)/shard_map/ppermute | solution.py:400
  51.0 10.7 %collective-permute-start.4 = (f32[33,48,128]{2,1,0:T(8,128)}, f32[33,48,128]{2,1,0:T(8,128)}, u32[]{:S(2)}, u32[]{:S(2)}) collective-permute-start(f32[33,48,128]{2,1,0:T(8,128)} %get-tuple-element.20), channel_id=1, source_target_pairs={{0,8},{1,9},{2,10},{3,11},{4,12},{5,13},{6,14},{7,15},{8,2},{9,3},... | collective-permute-start | bytes 2433032 | tf_op jit(solution)/shard_map/ppermute | solution.py:401
  93.3 14.4 %all-to-all-start.1 = ((f32[8,10,24,128]{3,2,1,0:T(8,128)}), f32[8,10,24,128]{3,2,1,0:T(8,128)S(1)}, u32[]{:S(2)}, u32[]{:S(2)}) async-start(f32[8,10,24,128]{3,2,1,0:T(8,128)} %steps.1), calls=%async_computation.1 | async-start | bytes 1966080 | tf_op jit(solution)/shard_map/all_to_all | solution.py:423
  107.7 7.8 %collective-permute-start.5 = (f32[4,10,24,128]{3,2,1,0:T(8,128)S(1)}, f32[4,10,24,128]{3,2,1,0:T(8,128)S(1)}, u32[]{:S(2)}, u32[]{:S(2)}) collective-permute-start(f32[4,10,24,128]{3,2,1,0:T(8,128)S(1)} %bitcast.30), channel_id=1, source_target_pairs={{0,8},{8,0},{16,24},{24,16},{32,40},{40,32},{48,56},{56,48},{64,72... | collective-permute-start | bytes 1474568 | tf_op jit(solution)/shard_map/ppermute | solution.py:427

commit v3 on v2

--- a/solution.py
+++ b/solution.py
@@ -120,7 +120,7 @@
             tail[w * 4 + c - 1] = jnp.where(inner, roll(two, 64 - SIDE), turned)
         return 0
 
-    lax.fori_loop(0, 8, pack, 0)
+    lax.fori_loop(0, 8, pack, 0, unroll=2)
     turned = roll(wall[...], 64)
     head[32] = turned
     tail[32] = turned
@@ -190,7 +190,7 @@
                 start[w * 20 + c * 4 + l] = pair[l]
         return 0
 
-    lax.fori_loop(0, 8, spread, 0)
+    lax.fori_loop(0, 8, spread, 0, unroll=2)
     for fetch in ends:
         fetch.wait()
     wall[0], wall[1] = widen(packed_wall[...], jnp.where(inner, head[32], tail[32]))
@@ -265,7 +265,7 @@
                 carry = advance(w, carry)
             return 0
 
-        lax.fori_loop(0, (high - low + 7) // 8, chunk, 0, unroll=2)
+        lax.fori_loop(0, (high - low + 7) // 8, chunk, 0, unroll=3)
 
     h = time_step
     bases = [start, buf_d, start]

time: 118 us -> 116 us (0.983)
  Pallas kernels: 37.2 us -> 35.7 us
    pallas_call x1, Pallas kernels: 30.9 us -> 29.7 us  [local(): pl.pallas_call(steps_kernel, out_shape=shape(8, 10, OWN_T, 128), in_specs...]
where the time goes in v3:
time: 116 us
  Pallas kernels  35.7 us (31%)
  blocking collectives  33.3 us (29%)
  waiting for transfers between devices  25.2 us (22%)
  starting transfers between devices  16 us (14%)
  local copies, waits for them, and re-layouts  5.26 us (5%)
    all_to_all x1, blocking collectives, local(): got = lax.all_to_all(pieces, 'wn', 0, 0, tiled=True)  33.3 us
    pallas_call x1, Pallas kernels, local(): pl.pallas_call(steps_kernel, out_shape=shape(8, 10, OWN_T, 128), in_specs...  29.7 us
    all_to_all x1, waiting for transfers between devices, local(): back = lax.all_to_all(done, 'wn', 0, 0, tiled=True)  10.7 us
    ppermute x1, waiting for transfers between devices, local(): head = lax.ppermute(head, ('az', 'wn'), [(j, i) for i, j in pairs])  10.3 us
    ppermute x1, starting transfers between devices, local(): other = lax.ppermute(other, 'az', swap)  6.29 us
    all_to_all x1, starting transfers between devices, local(): back = lax.all_to_all(done, 'wn', 0, 0, tiled=True)  3.73 us
    unnamed x12, local copies, waits for them, and re-layouts  3.46 us
    ppermute x1, waiting for transfers between devices, local(): lax.ppermute(send_pole, 'az', [(i, j ^ 1) for i, j in enumerate(opposite)])  2.62 us
  transfers between devices with their start and end apart: 7, of which 5 were waited for; matrix products, arithmetic and copies ran while one was open for 1% of the time, Pallas kernels for 0%

profile of v3, /device:TPU:1, one launch (start us, length us, event | category | flops | bytes accessed | tf_op | source)
XLA Modules:
  0.0 115.8 jit_solution(3532569570380969205)
XLA Ops:
  0.0 1.2 %copy-done.1 = f32[5,4,96,128]{3,2,1,0:T(8,128)S(1)} copy-done((f32[5,4,96,128]{3,2,1,0:T(8,128)S(1)}, f32[5,4,96,128]{3,2,1,0:T(8,128)}, u32[]{:S(2)}) %copy-start.1) | copy-done | bytes 983064
  1.2 0.8 copy-done.2
  2.0 0.8 copy-done.3
  2.8 0.7 copy-done.4
  3.5 1.4 %halves.1 = (f32[11,96,128]{2,1,0:T(8,128)S(1)}, f32[11,96,128]{2,1,0:T(8,128)S(1)}, f32[11,12,128]{2,1,0:T(8,128)S(1)}, f32[11,12,128]{2,1,0:T(8,128)S(1)}) custom-call(s32[1]{0:T(128)} %bitcast.1.core, f32[16]{0:T(128)S(1)} %copy-done.4, f32[20,96,128]{2,1,0:T(8,128)S(1)} %bitcast.29, s32[96,128]{1,0:T(8,128)S(1)} %copy-done.2, s32[96,128]{1,0:T(8,128)S(1)} %copy-done.3), custom_call_target="tpu_custom_call" | custom-call | tf_op jit(solution)/shard_map/halves/pallas_call | solution.py:338
  4.9 2.5 %collective-permute-start.1 = (f32[11,12,128]{2,1,0:T(8,128)S(1)}, f32[11,12,128]{2,1,0:T(8,128)S(1)}, u32[]{:S(2)}, u32[]{:S(2)}) collective-permute-start(f32[11,12,128]{2,1,0:T(8,128)S(1)} %get-tuple-element.15), channel_id=1, source_target_pairs={{0,64},{8,72},{16,80},{24,88},{32,96},{40,104},{48,112},{56,120},{... | collective-permute-start | bytes 202760 | tf_op jit(solution)/shard_map/ppermute | solution.py:358
  7.4 0.7 collective-permute-start.2
  8.1 0.3 collective-permute-start
  8.4 0.7 slice_bitcast_fusion.5
  9.5 0.2 collective-permute-done.1.keep_pole
  9.7 2.6 %collective-permute-done.2.got_pole = f32[11,12,128]{2,1,0:T(8,128)S(1)} collective-permute-done((f32[11,12,128]{2,1,0:T(8,128)S(1)}, f32[11,12,128]{2,1,0:T(8,128)S(1)}, u32[]{:S(2)}, u32[]{:S(2)}) %collective-permute-start.2) | collective-permute-done | bytes 67616 | tf_op jit(solution)/shard_map/ppermute | solution.py:359
  12.3 0.7 windows.1
  13.0 33.3 %all_to_all.10.got.got_far = f32[8,488,128]{2,1,0:T(8,128)S(1)} all-to-all(f32[8,488,128]{2,1,0:T(8,128)S(1)} %get-tuple-element.17), channel_id=1, replica_groups=mesh['az'=16,'wn'=8] {'wn'}, dimensions={0} | all-to-all | bytes 3997696 | tf_op jit(solution)/shard_map/all_to_all | solution.py:390
  46.3 2.1 %edges.1 = (f32[33,48,128]{2,1,0:T(8,128)}, f32[33,48,128]{2,1,0:T(8,128)}) custom-call(f32[8,488,128]{2,1,0:T(8,128)S(1)} %all_to_all.10.got.got_far, f32[48,128]{1,0:T(8,128)S(1)} %get-tuple-element.18.wall.packed_wall), custom_call_target="tpu_custom_call" | custom-call | tf_op jit(solution)/shard_map/edges/pallas_call | solution.py:391
  48.4 2.3 %collective-permute-start.3 = (f32[33,48,128]{2,1,0:T(8,128)}, f32[33,48,128]{2,1,0:T(8,128)S(1)}, u32[]{:S(2)}, u32[]{:S(2)}) collective-permute-start(f32[33,48,128]{2,1,0:T(8,128)} %get-tuple-element.19), channel_id=1, source_target_pairs={{8,0},{9,1},{10,2},{11,3},{12,4},{13,5},{14,6},{15,7},{2,8},{3,9},... | collective-permute-start | bytes 2433032 | tf_op jit(solution)/shard_map/ppermute | solution.py:400
  50.7 0.2 collective-permute-start.4
  51.2 10.3 %collective-permute-done.3.head_far = f32[33,48,128]{2,1,0:T(8,128)S(1)} collective-permute-done((f32[33,48,128]{2,1,0:T(8,128)}, f32[33,48,128]{2,1,0:T(8,128)S(1)}, u32[]{:S(2)}, u32[]{:S(2)}) %collective-permute-start.3) | collective-permute-done | bytes 811040 | tf_op jit(solution)/shard_map/ppermute | solution.py:400
  61.6 0.5 broadcast_in_dim.23.speed_far
  62.1 29.7 %steps.1 = f32[8,10,24,128]{3,2,1,0:T(8,128)} custom-call(f32[8,488,128]{2,1,0:T(8,128)} %copy-done, f32[33,48,128]{2,1,0:T(8,128)S(1)} %collective-permute-done.3.head_far, f32[33,48,128]{2,1,0:T(8,128)} %collective-permute-done.4.tail_far, f32[2,32,48,128]{3,2,1,0:T(8,128)S(1)} %broadcast_in_dim.23.speed_far, f32[48,128]{1,0:T(8,128)S(1)} %broadcast_in_dim.24.metric, ...), custom_call_target="tpu_custom_call" | custom-call | tf_op jit(solution)/shard_map/steps/pallas_call | solution.py:405
  91.8 3.7 %all-to-all-start.1 = ((f32[8,10,24,128]{3,2,1,0:T(8,128)}), f32[8,10,24,128]{3,2,1,0:T(8,128)S(1)}, u32[]{:S(2)}, u32[]{:S(2)}) async-start(f32[8,10,24,128]{3,2,1,0:T(8,128)} %steps.1), calls=%async_computation.1 | async-start | bytes 1966080 | tf_op jit(solution)/shard_map/all_to_all | solution.py:423
  95.5 10.7 %all-to-all-done.1.back = f32[8,10,24,128]{3,2,1,0:T(8,128)S(1)} async-done(((f32[8,10,24,128]{3,2,1,0:T(8,128)}), f32[8,10,24,128]{3,2,1,0:T(8,128)S(1)}, u32[]{:S(2)}, u32[]{:S(2)}) %all-to-all-start.1) | async-done | bytes 983072 | tf_op jit(solution)/shard_map/all_to_all | solution.py:423
  106.2 6.3 %collective-permute-start.5 = (f32[4,10,24,128]{3,2,1,0:T(8,128)S(1)}, f32[4,10,24,128]{3,2,1,0:T(8,128)S(1)}, u32[]{:S(2)}, u32[]{:S(2)}) collective-permute-start(f32[4,10,24,128]{3,2,1,0:T(8,128)S(1)} %bitcast.30), channel_id=1, source_target_pairs={{0,8},{8,0},{16,24},{24,16},{32,40},{40,32},{48,56},{56,48},{64,72... | collective-permute-start | bytes 1474568 | tf_op jit(solution)/shard_map/ppermute | solution.py:427
  112.6 1.4 %collective-permute-done.5.got = f32[4,10,24,128]{3,2,1,0:T(8,128)S(1)} collective-permute-done((f32[4,10,24,128]{3,2,1,0:T(8,128)S(1)}, f32[4,10,24,128]{3,2,1,0:T(8,128)S(1)}, u32[]{:S(2)}, u32[]{:S(2)}) %collective-permute-start.5) | collective-permute-done | bytes 491552 | tf_op jit(solution)/shard_map/ppermute | solution.py:427
  114.0 1.8 %join.1 = f32[5,4,96,128]{3,2,1,0:T(8,128)} custom-call(s32[2]{0:T(128)S(1)} %pad_add_fusion.place, f32[8,10,24,128]{3,2,1,0:T(8,128)S(1)} %all-to-all-done.1.back, f32[4,10,24,128]{3,2,1,0:T(8,128)S(1)} %collective-permute-done.5.got), custom_call_target="tpu_custom_call" | custom-call | tf_op jit(solution)/shard_map/join/pallas_call | solution.py:428
  (31 shorter events, 1.0 us)
Async XLA Ops:
  0.0 1.2 %copy-start.1 = (f32[5,4,96,128]{3,2,1,0:T(8,128)S(1)}, f32[5,4,96,128]{3,2,1,0:T(8,128)}, u32[]{:S(2)}) copy-start(f32[5,4,96,128]{3,2,1,0:T(8,128)} %param.6) | copy-start | bytes 2949124
  1.2 0.8 copy-start.2
  2.0 0.8 copy-start.3
  2.8 0.7 copy-start.4
  4.9 4.9 %collective-permute-start.1 = (f32[11,12,128]{2,1,0:T(8,128)S(1)}, f32[11,12,128]{2,1,0:T(8,128)S(1)}, u32[]{:S(2)}, u32[]{:S(2)}) collective-permute-start(f32[11,12,128]{2,1,0:T(8,128)S(1)} %get-tuple-element.15), channel_id=1, source_target_pairs={{0,64},{8,72},{16,80},{24,88},{32,96},{40,104},{48,112},{56,120},{... | collective-permute-start | bytes 202760 | tf_op jit(solution)/shard_map/ppermute | solution.py:358
  7.4 4.9 %collective-permute-start.2 = (f32[11,12,128]{2,1,0:T(8,128)S(1)}, f32[11,12,128]{2,1,0:T(8,128)S(1)}, u32[]{:S(2)}, u32[]{:S(2)}) collective-permute-start(f32[11,12,128]{2,1,0:T(8,128)S(1)} %get-tuple-element.16), channel_id=1, source_target_pairs={{0,72},{8,64},{16,88},{24,80},{32,104},{40,96},{48,120},{56,112},{... | collective-permute-start | bytes 202760 | tf_op jit(solution)/shard_map/ppermute | solution.py:359
  8.1 4.3 %collective-permute-start = (f32[11,96,128]{2,1,0:T(8,128)S(1)}, f32[11,96,128]{2,1,0:T(8,128)S(1)}, u32[]{:S(2)}, u32[]{:S(2)}) collective-permute-start(f32[11,96,128]{2,1,0:T(8,128)S(1)} %get-tuple-element.14), channel_id=1, source_target_pairs={{0,8},{8,0},{16,24},{24,16},{32,40},{40,32},{48,56},{56,48},{64,72... | collective-permute-start | bytes 1622024 | tf_op jit(solution)/shard_map/ppermute | solution.py:360
  46.3 15.8 %copy-start = (f32[8,488,128]{2,1,0:T(8,128)}, f32[8,488,128]{2,1,0:T(8,128)S(1)}, u32[]{:S(2)}) copy-start(f32[8,488,128]{2,1,0:T(8,128)S(1)} %all_to_all.10.got.got_far) | copy-start | bytes 5996548
  46.3 4.6 %copy-start.5 = (f32[96]{0:T(128)S(1)}, f32[96]{0:T(128)}, u32[]{:S(2)}) copy-start(f32[96]{0:T(128)} %param.8) | copy-start | bytes 1156
  48.4 13.1 %collective-permute-start.3 = (f32[33,48,128]{2,1,0:T(8,128)}, f32[33,48,128]{2,1,0:T(8,128)S(1)}, u32[]{:S(2)}, u32[]{:S(2)}) collective-permute-start(f32[33,48,128]{2,1,0:T(8,128)} %get-tuple-element.19), channel_id=1, source_target_pairs={{8,0},{9,1},{10,2},{11,3},{12,4},{13,5},{14,6},{15,7},{2,8},{3,9},... | collective-permute-start | bytes 2433032 | tf_op jit(solution)/shard_map/ppermute | solution.py:400
  50.7 10.7 %collective-permute-start.4 = (f32[33,48,128]{2,1,0:T(8,128)}, f32[33,48,128]{2,1,0:T(8,128)}, u32[]{:S(2)}, u32[]{:S(2)}) collective-permute-start(f32[33,48,128]{2,1,0:T(8,128)} %get-tuple-element.20), channel_id=1, source_target_pairs={{0,8},{1,9},{2,10},{3,11},{4,12},{5,13},{6,14},{7,15},{8,2},{9,3},... | collective-permute-start | bytes 2433032 | tf_op jit(solution)/shard_map/ppermute | solution.py:401
  91.8 14.4 %all-to-all-start.1 = ((f32[8,10,24,128]{3,2,1,0:T(8,128)}), f32[8,10,24,128]{3,2,1,0:T(8,128)S(1)}, u32[]{:S(2)}, u32[]{:S(2)}) async-start(f32[8,10,24,128]{3,2,1,0:T(8,128)} %steps.1), calls=%async_computation.1 | async-start | bytes 1966080 | tf_op jit(solution)/shard_map/all_to_all | solution.py:423
  106.2 7.8 %collective-permute-start.5 = (f32[4,10,24,128]{3,2,1,0:T(8,128)S(1)}, f32[4,10,24,128]{3,2,1,0:T(8,128)S(1)}, u32[]{:S(2)}, u32[]{:S(2)}) collective-permute-start(f32[4,10,24,128]{3,2,1,0:T(8,128)S(1)} %bitcast.30), channel_id=1, source_target_pairs={{0,8},{8,0},{16,24},{24,16},{32,40},{40,32},{48,56},{56,48},{64,72... | collective-permute-start | bytes 1474568 | tf_op jit(solution)/shard_map/ppermute | solution.py:427

commit v4 on v3

--- a/solution.py
+++ b/solution.py
@@ -236,7 +236,7 @@
                     div = ch * div
                     adv = hu * (after[0] - before[0]) + hv * (up[0] - down[0])
                     adv_p = hu * dr_p + hv * dt_p
-                    old = [read(base, w, c, l) for c in range(5)]
+                    old = now if base is source else [read(base, w, c, l) for c in range(5)]
                     new = [old[0] - adv - div, None, None, None, old[4] - adv_p - heat_ratio * div]
                     push = [None, ch * dr_p, ch * dt_p, cmm * da_p]
                     for c in (1, 2, 3):
@@ -351,7 +351,7 @@
             pltpu.VMEM((96, 128), jnp.int32),
             pltpu.SemaphoreType.DMA((3,)),
         ],
-        compiler_params=params(24),
+        compiler_params=params(52),
         name="halves",
     )(core[None].astype(jnp.int32), blow_table, state.reshape(20, 96, 128), seg_index, porous)
     swap = [(i, i ^ 1) for i in range(count)]

time: 116 us -> 115 us (level)
  local copies, waits for them, and re-layouts: 5.26 us -> 4.06 us
    unnamed x12 -> x10, local copies, waits for them, and re-layouts: 3.46 us -> 2.26 us
where the time goes in v4:
time: 115 us
  Pallas kernels  36.1 us (31%)
  blocking collectives  33.3 us (29%)
  waiting for transfers between devices  25.2 us (22%)
  starting transfers between devices  16 us (14%)
  local copies, waits for them, and re-layouts  4.06 us (4%)
    all_to_all x1, blocking collectives, local(): got = lax.all_to_all(pieces, 'wn', 0, 0, tiled=True)  33.3 us
    pallas_call x1, Pallas kernels, local(): pl.pallas_call(steps_kernel, out_shape=shape(8, 10, OWN_T, 128), in_specs...  29.4 us
    all_to_all x1, waiting for transfers between devices, local(): back = lax.all_to_all(done, 'wn', 0, 0, tiled=True)  10.7 us
    ppermute x1, waiting for transfers between devices, local(): head = lax.ppermute(head, ('az', 'wn'), [(j, i) for i, j in pairs])  10.3 us
    ppermute x1, starting transfers between devices, local(): other = lax.ppermute(other, 'az', swap)  6.29 us
    all_to_all x1, starting transfers between devices, local(): back = lax.all_to_all(done, 'wn', 0, 0, tiled=True)  3.73 us
    ppermute x1, waiting for transfers between devices, local(): lax.ppermute(send_pole, 'az', [(i, j ^ 1) for i, j in enumerate(opposite)])  2.62 us
    ppermute x1, starting transfers between devices, local(): keep_pole = lax.ppermute(keep_pole, 'az', list(enumerate(opposite)))  2.55 us
  transfers between devices with their start and end apart: 7, of which 5 were waited for; matrix products, arithmetic and copies ran while one was open for 1% of the time, Pallas kernels for 0%

profile of v4, /device:TPU:1, one launch (start us, length us, event | category | flops | bytes accessed | tf_op | source)
XLA Modules:
  0.0 115.1 jit_solution(7740418684743896934)
XLA Ops:
  0.0 0.8 copy-done.1
  0.8 0.8 copy-done.2
  1.6 0.7 copy-done.3
  2.3 2.2 %halves.1 = (f32[11,96,128]{2,1,0:T(8,128)S(1)}, f32[11,96,128]{2,1,0:T(8,128)S(1)}, f32[11,12,128]{2,1,0:T(8,128)S(1)}, f32[11,12,128]{2,1,0:T(8,128)S(1)}) custom-call(s32[1]{0:T(128)} %bitcast.1.core, f32[16]{0:T(128)S(1)} %copy-done.3, f32[20,96,128]{2,1,0:T(8,128)} %bitcast.29, s32[96,128]{1,0:T(8,128)S(1)} %copy-done.1, s32[96,128]{1,0:T(8,128)S(1)} %copy-done.2), custom_call_target="tpu_custom_call" | custom-call | tf_op jit(solution)/shard_map/halves/pallas_call | solution.py:338
  4.4 2.5 %collective-permute-start.1 = (f32[11,12,128]{2,1,0:T(8,128)S(1)}, f32[11,12,128]{2,1,0:T(8,128)S(1)}, u32[]{:S(2)}, u32[]{:S(2)}) collective-permute-start(f32[11,12,128]{2,1,0:T(8,128)S(1)} %get-tuple-element.15), channel_id=1, source_target_pairs={{0,64},{8,72},{16,80},{24,88},{32,96},{40,104},{48,112},{56,120},{... | collective-permute-start | bytes 202760 | tf_op jit(solution)/shard_map/ppermute | solution.py:358
  7.0 0.7 collective-permute-start.2
  7.6 0.3 collective-permute-start
  7.9 0.7 slice_bitcast_fusion.5
  9.1 0.2 collective-permute-done.1.keep_pole
  9.3 2.6 %collective-permute-done.2.got_pole = f32[11,12,128]{2,1,0:T(8,128)S(1)} collective-permute-done((f32[11,12,128]{2,1,0:T(8,128)S(1)}, f32[11,12,128]{2,1,0:T(8,128)S(1)}, u32[]{:S(2)}, u32[]{:S(2)}) %collective-permute-start.2) | collective-permute-done | bytes 67616 | tf_op jit(solution)/shard_map/ppermute | solution.py:359
  11.9 0.7 windows.1
  12.6 33.3 %all_to_all.10.got.got_far = f32[8,488,128]{2,1,0:T(8,128)S(1)} all-to-all(f32[8,488,128]{2,1,0:T(8,128)S(1)} %get-tuple-element.17), channel_id=1, replica_groups=mesh['az'=16,'wn'=8] {'wn'}, dimensions={0} | all-to-all | bytes 3997696 | tf_op jit(solution)/shard_map/all_to_all | solution.py:390
  45.9 2.1 %edges.1 = (f32[33,48,128]{2,1,0:T(8,128)}, f32[33,48,128]{2,1,0:T(8,128)}) custom-call(f32[8,488,128]{2,1,0:T(8,128)S(1)} %all_to_all.10.got.got_far, f32[48,128]{1,0:T(8,128)S(1)} %get-tuple-element.18.wall.packed_wall), custom_call_target="tpu_custom_call" | custom-call | tf_op jit(solution)/shard_map/edges/pallas_call | solution.py:391
  48.0 2.3 %collective-permute-start.3 = (f32[33,48,128]{2,1,0:T(8,128)}, f32[33,48,128]{2,1,0:T(8,128)S(1)}, u32[]{:S(2)}, u32[]{:S(2)}) collective-permute-start(f32[33,48,128]{2,1,0:T(8,128)} %get-tuple-element.19), channel_id=1, source_target_pairs={{8,0},{9,1},{10,2},{11,3},{12,4},{13,5},{14,6},{15,7},{2,8},{3,9},... | collective-permute-start | bytes 2433032 | tf_op jit(solution)/shard_map/ppermute | solution.py:400
  50.3 0.2 collective-permute-start.4
  50.5 0.1 rev.11
  50.8 10.3 %collective-permute-done.3.head_far = f32[33,48,128]{2,1,0:T(8,128)S(1)} collective-permute-done((f32[33,48,128]{2,1,0:T(8,128)}, f32[33,48,128]{2,1,0:T(8,128)S(1)}, u32[]{:S(2)}, u32[]{:S(2)}) %collective-permute-start.3) | collective-permute-done | bytes 811040 | tf_op jit(solution)/shard_map/ppermute | solution.py:400
  61.2 0.5 broadcast_in_dim.23.speed_far
  61.7 29.4 %steps.1 = f32[8,10,24,128]{3,2,1,0:T(8,128)} custom-call(f32[8,488,128]{2,1,0:T(8,128)} %copy-done, f32[33,48,128]{2,1,0:T(8,128)S(1)} %collective-permute-done.3.head_far, f32[33,48,128]{2,1,0:T(8,128)} %collective-permute-done.4.tail_far, f32[2,32,48,128]{3,2,1,0:T(8,128)S(1)} %broadcast_in_dim.23.speed_far, f32[48,128]{1,0:T(8,128)S(1)} %broadcast_in_dim.24.metric, ...), custom_call_target="tpu_custom_call" | custom-call | tf_op jit(solution)/shard_map/steps/pallas_call | solution.py:405
  91.1 3.7 %all-to-all-start.1 = ((f32[8,10,24,128]{3,2,1,0:T(8,128)}), f32[8,10,24,128]{3,2,1,0:T(8,128)S(1)}, u32[]{:S(2)}, u32[]{:S(2)}) async-start(f32[8,10,24,128]{3,2,1,0:T(8,128)} %steps.1), calls=%async_computation.1 | async-start | bytes 1966080 | tf_op jit(solution)/shard_map/all_to_all | solution.py:423
  94.8 10.7 %all-to-all-done.1.back = f32[8,10,24,128]{3,2,1,0:T(8,128)S(1)} async-done(((f32[8,10,24,128]{3,2,1,0:T(8,128)}), f32[8,10,24,128]{3,2,1,0:T(8,128)S(1)}, u32[]{:S(2)}, u32[]{:S(2)}) %all-to-all-start.1) | async-done | bytes 983072 | tf_op jit(solution)/shard_map/all_to_all | solution.py:423
  105.5 6.3 %collective-permute-start.5 = (f32[4,10,24,128]{3,2,1,0:T(8,128)S(1)}, f32[4,10,24,128]{3,2,1,0:T(8,128)S(1)}, u32[]{:S(2)}, u32[]{:S(2)}) collective-permute-start(f32[4,10,24,128]{3,2,1,0:T(8,128)S(1)} %bitcast.30), channel_id=1, source_target_pairs={{0,8},{8,0},{16,24},{24,16},{32,40},{40,32},{48,56},{56,48},{64,72... | collective-permute-start | bytes 1474568 | tf_op jit(solution)/shard_map/ppermute | solution.py:427
  111.9 1.4 %collective-permute-done.5.got = f32[4,10,24,128]{3,2,1,0:T(8,128)S(1)} collective-permute-done((f32[4,10,24,128]{3,2,1,0:T(8,128)S(1)}, f32[4,10,24,128]{3,2,1,0:T(8,128)S(1)}, u32[]{:S(2)}, u32[]{:S(2)}) %collective-permute-start.5) | collective-permute-done | bytes 491552 | tf_op jit(solution)/shard_map/ppermute | solution.py:427
  113.3 1.8 %join.1 = f32[5,4,96,128]{3,2,1,0:T(8,128)} custom-call(s32[2]{0:T(128)S(1)} %pad_add_fusion.place, f32[8,10,24,128]{3,2,1,0:T(8,128)S(1)} %all-to-all-done.1.back, f32[4,10,24,128]{3,2,1,0:T(8,128)S(1)} %collective-permute-done.5.got), custom_call_target="tpu_custom_call" | custom-call | tf_op jit(solution)/shard_map/join/pallas_call | solution.py:428
  (29 shorter events, 0.9 us)
Async XLA Ops:
  0.0 0.8 copy-start.1
  0.8 0.8 copy-start.2
  1.6 0.7 copy-start.3
  4.4 4.9 %collective-permute-start.1 = (f32[11,12,128]{2,1,0:T(8,128)S(1)}, f32[11,12,128]{2,1,0:T(8,128)S(1)}, u32[]{:S(2)}, u32[]{:S(2)}) collective-permute-start(f32[11,12,128]{2,1,0:T(8,128)S(1)} %get-tuple-element.15), channel_id=1, source_target_pairs={{0,64},{8,72},{16,80},{24,88},{32,96},{40,104},{48,112},{56,120},{... | collective-permute-start | bytes 202760 | tf_op jit(solution)/shard_map/ppermute | solution.py:358
  7.0 4.9 %collective-permute-start.2 = (f32[11,12,128]{2,1,0:T(8,128)S(1)}, f32[11,12,128]{2,1,0:T(8,128)S(1)}, u32[]{:S(2)}, u32[]{:S(2)}) collective-permute-start(f32[11,12,128]{2,1,0:T(8,128)S(1)} %get-tuple-element.16), channel_id=1, source_target_pairs={{0,72},{8,64},{16,88},{24,80},{32,104},{40,96},{48,120},{56,112},{... | collective-permute-start | bytes 202760 | tf_op jit(solution)/shard_map/ppermute | solution.py:359
  7.6 4.3 %collective-permute-start = (f32[11,96,128]{2,1,0:T(8,128)S(1)}, f32[11,96,128]{2,1,0:T(8,128)S(1)}, u32[]{:S(2)}, u32[]{:S(2)}) collective-permute-start(f32[11,96,128]{2,1,0:T(8,128)S(1)} %get-tuple-element.14), channel_id=1, source_target_pairs={{0,8},{8,0},{16,24},{24,16},{32,40},{40,32},{48,56},{56,48},{64,72... | collective-permute-start | bytes 1622024 | tf_op jit(solution)/shard_map/ppermute | solution.py:360
  45.9 15.8 %copy-start = (f32[8,488,128]{2,1,0:T(8,128)}, f32[8,488,128]{2,1,0:T(8,128)S(1)}, u32[]{:S(2)}) copy-start(f32[8,488,128]{2,1,0:T(8,128)S(1)} %all_to_all.10.got.got_far) | copy-start | bytes 5996548
  45.9 4.6 %copy-start.4 = (f32[96]{0:T(128)S(1)}, f32[96]{0:T(128)}, u32[]{:S(2)}) copy-start(f32[96]{0:T(128)} %param.8) | copy-start | bytes 1156
  48.0 13.1 %collective-permute-start.3 = (f32[33,48,128]{2,1,0:T(8,128)}, f32[33,48,128]{2,1,0:T(8,128)S(1)}, u32[]{:S(2)}, u32[]{:S(2)}) collective-permute-start(f32[33,48,128]{2,1,0:T(8,128)} %get-tuple-element.19), channel_id=1, source_target_pairs={{8,0},{9,1},{10,2},{11,3},{12,4},{13,5},{14,6},{15,7},{2,8},{3,9},... | collective-permute-start | bytes 2433032 | tf_op jit(solution)/shard_map/ppermute | solution.py:400
  50.3 10.7 %collective-permute-start.4 = (f32[33,48,128]{2,1,0:T(8,128)}, f32[33,48,128]{2,1,0:T(8,128)}, u32[]{:S(2)}, u32[]{:S(2)}) collective-permute-start(f32[33,48,128]{2,1,0:T(8,128)} %get-tuple-element.20), channel_id=1, source_target_pairs={{0,8},{1,9},{2,10},{3,11},{4,12},{5,13},{6,14},{7,15},{8,2},{9,3},... | collective-permute-start | bytes 2433032 | tf_op jit(solution)/shard_map/ppermute | solution.py:401
  91.1 14.4 %all-to-all-start.1 = ((f32[8,10,24,128]{3,2,1,0:T(8,128)}), f32[8,10,24,128]{3,2,1,0:T(8,128)S(1)}, u32[]{:S(2)}, u32[]{:S(2)}) async-start(f32[8,10,24,128]{3,2,1,0:T(8,128)} %steps.1), calls=%async_computation.1 | async-start | bytes 1966080 | tf_op jit(solution)/shard_map/all_to_all | solution.py:423
  105.5 7.8 %collective-permute-start.5 = (f32[4,10,24,128]{3,2,1,0:T(8,128)S(1)}, f32[4,10,24,128]{3,2,1,0:T(8,128)S(1)}, u32[]{:S(2)}, u32[]{:S(2)}) collective-permute-start(f32[4,10,24,128]{3,2,1,0:T(8,128)S(1)} %bitcast.30), channel_id=1, source_target_pairs={{0,8},{8,0},{16,24},{24,16},{32,40},{40,32},{48,56},{56,48},{64,72... | collective-permute-start | bytes 1474568 | tf_op jit(solution)/shard_map/ppermute | solution.py:427
